TPU v7x, 128 devices: a whole 4x4x4 slice. The times are simulated.
128 devices in a mesh: pipe: 2 (over y_lo), shard: 32 (over z, x, core), tensor: 2 (over y_hi).
Axes of the slice: x: 4, y: 4 (y_hi: 2, y_lo: 2; y = y_hi * 2 + y_lo), z: 4, core: 2. Of those that a mesh axis runs over, the one named last changes fastest.
Arguments:
- clip_frames: bfloat16 [4, 6144, 768], P(None, 'shard'), may hold values from -6 to 6
- out_cotangent: bfloat16 [4, 6144, 768], P(None, 'shard'), may hold values from -6 to 6
- clip_lengths: int32 [4, 32], P(None, 'shard'), may hold values from 48 to 192, as said below
- query_weight: bfloat16 [2, 768, 768], P('pipe', 'shard', 'tensor'), may hold values from -0.21875 to 0.21875
- key_weight: bfloat16 [2, 768, 768], P('pipe', 'shard', 'tensor'), may hold values from -0.21875 to 0.21875
- value_weight: bfloat16 [2, 768, 768], P('pipe', 'shard', 'tensor'), may hold values from -0.21875 to 0.21875
- output_weight: bfloat16 [2, 768, 768], P('pipe', 'shard', 'tensor'), may hold values from -0.875 to 0.875
- up_weight: bfloat16 [2, 768, 3072], P('pipe', 'shard', 'tensor'), may hold values from -0.21875 to 0.21875
- down_weight: bfloat16 [2, 768, 3072], P('pipe', 'shard', 'tensor'), may hold values from -0.15625 to 0.15625
- query_bias: bfloat16 [2, 64, 12], P('pipe', 'shard', 'tensor'), may hold values from -3 to 3
- value_bias: bfloat16 [2, 64, 12], P('pipe', 'shard', 'tensor'), may hold values from -3 to 3
- output_bias: bfloat16 [2, 768], P('pipe', 'shard'), may hold values from -3 to 3
- up_bias: bfloat16 [2, 64, 48], P('pipe', 'shard', 'tensor'), may hold values from -3 to 3
- down_bias: bfloat16 [2, 768], P('pipe', 'shard'), may hold values from -3 to 3
- first_gain: bfloat16 [2, 768], P('pipe', 'shard'), may hold values from 0.5 to 1.5
- first_shift: bfloat16 [2, 768], P('pipe', 'shard'), may hold values from -2 to 2
- second_gain: bfloat16 [2, 768], P('pipe', 'shard'), may hold values from 0.5 to 1.5
- second_shift: bfloat16 [2, 768], P('pipe', 'shard'), may hold values from -2 to 2
Outputs:
- section_output: bfloat16 [2, 4, 6144, 768], P('pipe', None, 'shard')
- input_grad: bfloat16 [2, 4, 6144, 768], P('pipe', None, 'shard')
- query_weight_grad: float32 [2, 768, 768], P('pipe', 'shard', 'tensor')
- key_weight_grad: float32 [2, 768, 768], P('pipe', 'shard', 'tensor')
- value_weight_grad: float32 [2, 768, 768], P('pipe', 'shard', 'tensor')
- output_weight_grad: float32 [2, 768, 768], P('pipe', 'shard', 'tensor')
- up_weight_grad: float32 [2, 768, 3072], P('pipe', 'shard', 'tensor')
- down_weight_grad: float32 [2, 768, 3072], P('pipe', 'shard', 'tensor')
- query_bias_grad: float32 [2, 64, 12], P('pipe', 'shard', 'tensor')
- value_bias_grad: float32 [2, 64, 12], P('pipe', 'shard', 'tensor')
- output_bias_grad: float32 [2, 768], P('pipe', 'shard')
- up_bias_grad: float32 [2, 64, 48], P('pipe', 'shard', 'tensor')
- down_bias_grad: float32 [2, 768], P('pipe', 'shard')
- first_gain_grad: float32 [2, 768], P('pipe', 'shard')
- first_shift_grad: float32 [2, 768], P('pipe', 'shard')
- second_gain_grad: float32 [2, 768], P('pipe', 'shard')
- second_shift_grad: float32 [2, 768], P('pipe', 'shard')
Inputs may be any that keep to these rules, and one draw needn't show every extreme that they name: `clip_lengths`: frames of a clip at or past its length are padding and are not attended to as keys; some clip of the batch has all 192 frames.
All inputs are finite; a program needn't handle non-finite values.
Results may differ from a plain program's by a relative error of at most 0.033.
Values may be sent and summed in bfloat16 or wider, within the bound.
No kernel may reach another device: no remote copies, remote signals or barrier semaphores. Data moves between devices by JAX's collectives and lax.ppermute only.
A program may use at most 192 MiB of HBM per device.

v0:
```python
import functools

import jax
import jax.numpy as jnp
import numpy as np
from jax import lax
from jax.experimental import pallas as pl
from jax.experimental.pallas import tpu as pltpu
from jax.sharding import Mesh
from jax.sharding import PartitionSpec as P

HEAD = 64
bf16 = jnp.bfloat16
f32 = jnp.float32

half_root = 0.7071067811865476
gauss_factor = 0.3989422804014327


EXCHANGES = {"xu": ("x", 4, 1), "xv": ("x", 4, 3), "zu": ("z", 4, 1), "zv": ("z", 4, 3), "c": ("core", 2, 1)}
BLOCK_BITS = ("zv", "zu", "xv", "xu")
BIT_MASK = {"xu": 1, "xv": 3, "zu": 4, "zv": 12}
ORDERS = (
    ("xu", "xv", "zu", "zv"),
    ("xv", "xu", "zv", "zu"),
    ("zu", "zv", "xu", "xv"),
    ("zv", "zu", "xv", "xu"),
)
MASKS = np.zeros(16, np.int32)
for _index in range(16):
    for _place, _bit in enumerate(BLOCK_BITS):
        if (_index >> (3 - _place)) & 1:
            MASKS[_index] ^= BIT_MASK[_bit]
ATTN_COLS = (384, 384, 384, 512)


def block_place(part, index):
    place = 0
    for step in range(4):
        if (index >> step) & 1:
            place += 8 >> BLOCK_BITS.index(ORDERS[part][step])
    return place


def dot(left_side, right_side):
    return lax.dot_general(left_side, right_side, (((1,), (0,)), ((), ())), preferred_element_type=f32)


def dot_rows(left_side, right_side):
    return lax.dot_general(left_side, right_side, (((0,), (0,)), ((), ())), preferred_element_type=f32)


def dot_cols(left_side, right_side):
    return lax.dot_general(left_side, right_side, (((1,), (1,)), ((), ())), preferred_element_type=f32)


def norm_parts(values):
    center = values - jnp.mean(values, -1, keepdims=True)
    rescale = lax.rsqrt(jnp.mean(center * center, -1, keepdims=True) + 1e-05)
    return center * rescale, rescale


def norm_backward(grad_rows, normed, rescale, norm_gain):
    scaled = grad_rows * norm_gain
    inner = (
        scaled
        - jnp.mean(scaled, -1, keepdims=True)
        - normed * jnp.mean(scaled * normed, -1, keepdims=True)
    )
    return rescale * inner


def put_blocks(out_ref, part, half, slot, start, value, where_ref):
    value = value.astype(bf16)
    for index in range(16):
        if where_ref is None:
            place = 48 * block_place(part, index)
            block = out_ref.at[index] if slot is None else out_ref.at[slot, index]
        else:
            place = 48 * index
            block = out_ref.at[2 * (where_ref[0] ^ int(MASKS[index])) + (where_ref[1] ^ half)]
        block[:, start : start + value.shape[1]] = value[place : place + 48]


def attention_forward_kernel(
    length_ref, x_ref, own_ref, peer_ref, place_ref,
    middle_ref, heads_ref, soft_ref, mixed_ref, vec_ref, up_bias_ref,
):
    length = length_ref[0]
    vec_ref[0:6] = own_ref[:, 1536:].astype(f32).T[0:6]
    units = []
    for weight_ref in (own_ref, peer_ref):
        rows = dot(place_ref[...], weight_ref[:, 1536:]).T
        units += [rows[:64], rows[64:]]
    for row, first in ((6, 8), (7, 11)):
        pieces = [rows[first + i : first + i + 1] for rows in units for i in range(3)]
        vec_ref[row : row + 1] = jnp.concatenate(pieces, 1)
    pieces = [rows[14 + i : 15 + i] for rows in units for i in range(12)]
    for i in range(24):
        up_bias_ref[0:1, 128 * i : 128 * i + 128] = jnp.concatenate(pieces[2 * i : 2 * i + 2], 1)
    normed, _ = norm_parts(x_ref[...].astype(f32))
    normed_b = (normed * vec_ref[2:3] + vec_ref[3:4]).astype(bf16)
    for j in range(3):
        for half, weight_ref in enumerate((own_ref, peer_ref)):
            cols = slice(384 * half, 384 * half + 384)
            rows = dot(normed_b, weight_ref[:, 384 * j : 384 * j + 384])
            if j != 1:
                rows = rows + vec_ref[6 + j // 2 : 7 + j // 2, cols]
            heads_ref[j, :, cols] = rows.astype(bf16)
    count = x_ref.shape[0]
    live_keys = lax.broadcasted_iota(jnp.int32, (count, count), 1) < length
    for pair in range(6):
        both = []
        for head in (2 * pair, 2 * pair + 1):
            cols = slice(HEAD * head, HEAD * head + HEAD)
            scores = dot_cols(heads_ref[0, :, cols], heads_ref[1, :, cols]) * HEAD ** (-0.5)
            scores = jnp.where(live_keys, scores, -1e30)
            powers = jnp.exp(scores - jnp.max(scores, -1, keepdims=True))
            soft = powers / jnp.sum(powers, -1, keepdims=True)
            soft_ref[head] = soft
            both.append(dot(soft.astype(bf16), heads_ref[2, :, cols]))
        mixed_ref[:, 128 * pair : 128 * pair + 128] = jnp.concatenate(both, 1).astype(bf16)
    total = dot_cols(mixed_ref[:, :384], own_ref[:, 1152:1536])
    total = total + dot_cols(mixed_ref[:, 384:], peer_ref[:, 1152:1536])
    middle_ref[...] = x_ref[...].astype(f32) + total + vec_ref[0:1]


def units_forward_kernel(middle_ref, own_ref, peer_ref, vec_ref, up_bias_ref, result_ref, active_ref, slope_ref):
    middle = middle_ref[...]
    normed, _ = norm_parts(middle)
    normed_b = (normed * vec_ref[4:5] + vec_ref[5:6]).astype(bf16)
    total = middle + vec_ref[1:2]
    for half, weight_ref in enumerate((own_ref, peer_ref)):
        for j in range(2):
            cols = slice(768 * (2 * half + j), 768 * (2 * half + j) + 768)
            pre_active = dot(normed_b, weight_ref[j]) + up_bias_ref[0:1, cols]
            below = 0.5 * (1.0 + lax.erf(pre_active * half_root))
            active_b = (pre_active * below).astype(bf16)
            active_ref[:, cols] = active_b
            slope_ref[:, cols] = below + pre_active * jnp.exp(-0.5 * pre_active * pre_active) * gauss_factor
            total = total + dot_cols(active_b, weight_ref[2 + j])
    result_ref[...] = total.astype(bf16)


def units_backward_kernel(placed, *refs):
    where_ref, refs = (refs[0], refs[1:]) if placed else (None, refs)
    grad_ref, middle_ref, active_ref, slope_ref, own_ref, peer_ref, vec_ref = refs[:7]
    grad_middle_ref, vec_grad_ref, up_bias_grad_ref, grad_own_ref = refs[7:11]
    grad_peer_ref = grad_own_ref if placed else refs[11]
    grad_b = grad_ref[...]
    grad_rows = grad_b.astype(f32)
    normed, rescale = norm_parts(middle_ref[...])
    normed_b = (normed * vec_ref[4:5] + vec_ref[5:6]).astype(bf16)
    normed_t = normed_b.T
    grad_t = grad_b.T
    grad_normed = None
    for half, weight_ref, out_ref in ((1, peer_ref, grad_peer_ref), (0, own_ref, grad_own_ref)):
        for j in range(2):
            cols = slice(768 * (2 * half + j), 768 * (2 * half + j) + 768)
            slot, start = (None, 768 * j) if placed else (j, 0)
            value = dot(grad_t, active_ref[:, cols])
            put_blocks(out_ref, 2 + j, half, None if placed else 2 + j, 1536 + start if placed else 0, value, where_ref)
            grad_upper = (dot(grad_b, weight_ref[2 + j]) * slope_ref[:, cols]).astype(bf16)
            up_bias_grad_ref[0:1, cols] = jnp.sum(grad_upper.astype(f32), 0, keepdims=True)
            put_blocks(out_ref, j, half, slot, start, dot(normed_t, grad_upper), where_ref)
            term = dot_cols(grad_upper, weight_ref[j])
            grad_normed = term if grad_normed is None else grad_normed + term
    grad_middle = grad_rows + norm_backward(grad_normed, normed, rescale, vec_ref[4:5])
    grad_middle_ref[...] = grad_middle
    vec_grad_ref[...] = jnp.zeros_like(vec_grad_ref)
    vec_grad_ref[0:1] = jnp.sum(grad_middle, 0, keepdims=True)
    vec_grad_ref[1:2] = jnp.sum(grad_rows, 0, keepdims=True)
    vec_grad_ref[4:5] = jnp.sum(grad_normed * normed, 0, keepdims=True)
    vec_grad_ref[5:6] = jnp.sum(grad_normed, 0, keepdims=True)


def attention_backward_kernel(placed, *refs):
    where_ref, refs = (refs[0], refs[1:]) if placed else (None, refs)
    grad_ref, x_ref, heads_ref, soft_ref, mixed_ref, own_ref, peer_ref, vec_ref = refs[:8]
    units_vec_ref, up_bias_grad_ref, place_ref, grad_in_ref, grad_own_ref = refs[8:13]
    grad_peer_ref = grad_own_ref if placed else refs[13]
    grad_mixed_ref, grad_heads_ref, cols_ref, small_ref = refs[-4:]
    grad_b = grad_ref[...].astype(bf16)
    grad_t = grad_b.T
    grad_mixed_ref[:, :384] = dot(grad_b, own_ref[:, 1152:1536]).astype(bf16)
    grad_mixed_ref[:, 384:] = dot(grad_b, peer_ref[:, 1152:1536]).astype(bf16)
    factor = HEAD ** (-0.5)
    for pair in range(6):
        found = ([], [], [])
        for head in (2 * pair, 2 * pair + 1):
            cols = slice(HEAD * head, HEAD * head + HEAD)
            soft = soft_ref[head]
            grad_head = grad_mixed_ref[:, cols]
            grad_soft = dot_cols(grad_head, heads_ref[2, :, cols])
            inner = jnp.sum(grad_soft * soft, -1, keepdims=True)
            grad_scores = (soft * (grad_soft - inner)).astype(bf16)
            found[0].append(dot(grad_scores, heads_ref[1, :, cols]) * factor)
            found[1].append(dot_rows(grad_scores, heads_ref[0, :, cols]) * factor)
            found[2].append(dot_rows(soft.astype(bf16), grad_head))
        for j in range(3):
            grad_heads_ref[j, :, 128 * pair : 128 * pair + 128] = jnp.concatenate(found[j], 1).astype(bf16)
    normed, rescale = norm_parts(x_ref[...].astype(f32))
    normed_b = (normed * vec_ref[2:3] + vec_ref[3:4]).astype(bf16)
    normed_t = normed_b.T
    grad_normed = None
    for half, weight_ref, out_ref in ((1, peer_ref, grad_peer_ref), (0, own_ref, grad_own_ref)):
        for j in range(3):
            rows = grad_heads_ref[j, :, 384 * half : 384 * half + 384]
            put_blocks(out_ref, j, half, None, 384 * j, dot(normed_t, rows), where_ref)
            term = dot_cols(rows, weight_ref[:, 384 * j : 384 * j + 384])
            grad_normed = term if grad_normed is None else grad_normed + term
    grad_in = grad_ref[...] + norm_backward(grad_normed, normed, rescale, vec_ref[2:3])
    grad_in_ref[...] = grad_in.astype(bf16)
    cols_ref[...] = jnp.zeros_like(cols_ref)
    cols_ref[0:2] = units_vec_ref[0:2]
    cols_ref[2:3] = jnp.sum(grad_normed * normed, 0, keepdims=True)
    cols_ref[3:4] = jnp.sum(grad_normed, 0, keepdims=True)
    cols_ref[4:6] = units_vec_ref[4:6]
    cols_ref[64:70] = cols_ref[0:6]
    cols = cols_ref[...].T
    query_bias = jnp.sum(grad_heads_ref[0].astype(f32), 0, keepdims=True)
    value_bias = jnp.sum(grad_heads_ref[2].astype(f32), 0, keepdims=True)
    for half, out_ref in ((1, grad_peer_ref), (0, grad_own_ref)):
        small_ref[...] = jnp.zeros_like(small_ref)
        for t in range(2):
            base = 64 * t
            for i in range(3):
                at = HEAD * (6 * half + 3 * t + i)
                small_ref[base + 8 + i : base + 9 + i] = query_bias[:, at : at + HEAD]
                small_ref[base + 11 + i : base + 12 + i] = value_bias[:, at : at + HEAD]
            for i in range(12):
                at = HEAD * (24 * half + 12 * t + i)
                small_ref[base + 14 + i : base + 15 + i] = up_bias_grad_ref[0:1, at : at + HEAD]
        small = dot_cols(place_ref[...], small_ref[...].astype(bf16)) + cols
        weight = dot(grad_t, mixed_ref[:, 384 * half : 384 * half + 384])
        put_blocks(out_ref, 3, half, None, 1152, jnp.concatenate([weight, small], 1), where_ref)


def kernel_call(kernel, name, inputs, outputs, scratch=(), scalar=False, blocks=None, large=True):
    whole = pl.BlockSpec(memory_space=pltpu.VMEM)
    specs = [whole] * len(inputs)
    out_specs = [whole] * len(outputs)
    if blocks is not None:
        specs = [pl.BlockSpec(shape, lambda i, at=at: at) for shape, at in blocks]
        out_specs = [pl.BlockSpec(shape, lambda i, n=len(shape): (0,) * n) for shape, _ in outputs]
    if scalar:
        specs[0] = pl.BlockSpec(memory_space=pltpu.SMEM)
    shapes = [jax.ShapeDtypeStruct(shape, dtype) for shape, dtype in outputs]
    return pl.pallas_call(
        kernel,
        name=name,
        out_shape=shapes,
        in_specs=specs,
        out_specs=out_specs,
        grid=() if blocks is None else (1,),
        scratch_shapes=list(scratch),
        cost_estimate=pl.CostEstimate(flops=1, bytes_accessed=1, transcendentals=0),
        compiler_params=pltpu.CompilerParams(vmem_limit_bytes=52 * 2**20 if large else None),
    )(*inputs)


ROWS = (192, 768)
HEADS_SHAPE = (3, 192, 768)
UNITS_SHAPE = (4, 16, 48, 768)
ATTN_SHAPE = (16, 48, 1664)
PLACED_UNITS = (32, 48, 3072)
PLACED_ATTN = (32, 48, 1664)


def attention_forward(length, x, attn, place_units):
    own, peer = attn
    return kernel_call(
        attention_forward_kernel, "attention_forward",
        [length, x, own, peer, place_units],
        [(ROWS, f32), (HEADS_SHAPE, bf16), ((12, 192, 192), f32), (ROWS, bf16), ((8, 768), f32), ((1, 3072), f32)],
        scalar=True,
    )


def units_forward(middle, units, vec, up_bias):
    own, peer = units
    return kernel_call(
        units_forward_kernel, "units_forward", [middle, own, peer, vec, up_bias],
        [(ROWS, bf16), ((192, 3072), bf16), ((192, 3072), f32)],
    )


def units_backward(grad_b, middle, active, slope, units, vec, where=None):
    own, peer = units
    placed = where is not None
    shapes = [PLACED_UNITS] if placed else [UNITS_SHAPE] * 2
    return kernel_call(
        functools.partial(units_backward_kernel, placed), "units_backward",
        [where] * placed + [grad_b, middle, active, slope, own, peer, vec],
        [(ROWS, f32), ((8, 768), f32), ((1, 3072), f32)] + [(shape, bf16) for shape in shapes], scalar=placed,
    )


def attention_backward(
    grad_middle, x, heads, soft, mixed, attn, vec, units_vec, up_bias_grad, place_units, where=None
):
    own, peer = attn
    placed = where is not None
    shapes = [PLACED_ATTN] if placed else [ATTN_SHAPE] * 2
    return kernel_call(
        functools.partial(attention_backward_kernel, placed), "attention_backward",
        [where] * placed
        + [grad_middle, x, heads, soft, mixed, own, peer, vec, units_vec, up_bias_grad, place_units],
        [(ROWS, bf16)] + [(shape, bf16) for shape in shapes], scalar=placed,
        scratch=[
            pltpu.VMEM(ROWS, bf16), pltpu.VMEM(HEADS_SHAPE, bf16), pltpu.VMEM((128, 768), f32),
            pltpu.VMEM((128, 64), f32),
        ],
    )


def exchange(value, bit):
    axis, size, flip = EXCHANGES[bit]
    return lax.ppermute(value, axis, [(i, i ^ flip) for i in range(size)])


def exchange_pipe(value):
    return lax.ppermute(value, "pipe", [(0, 1), (1, 0)])


def exchange_both(value):
    return lax.ppermute(value, ("pipe", "tensor"), [(i, i ^ 3) for i in range(4)])


def exchange_tensor(value):
    return lax.ppermute(value, "tensor", [(0, 1), (1, 0)])


def pin(*values):
    return lax.optimization_barrier(values)


def assemble_kernel(slots, *refs):
    count = len(slots)
    out = refs[-1]
    for number, (part, slot, start) in enumerate(slots):
        for index in range(16):
            rows = refs[number + (0 if index < 8 else count)][index % 8]
            place = slice(48 * block_place(part, index), 48 * block_place(part, index) + 48)
            cols = slice(start, start + rows.shape[1])
            if slot is None:
                out[place, cols] = rows
            else:
                out[slot, place, cols] = rows


def assemble(held, got, units):
    inputs, blocks, slots = [], [], []
    for part in range(4):
        width = (384, 256)[part // 3] if units else ATTN_COLS[part]
        first = ATTN_COLS[part] // width if units else 0
        for k in range(768 // width if units else 1):
            inputs.append(part)
            blocks.append(((8, 48, width), (0, 0, first + k)))
            slots.append((part, part, width * k) if units else (part, None, 384 * part))
    arrays = [held[part] for part in inputs] + [got[part] for part in inputs]
    shape = (4, 768, 768) if units else (768, 1664)
    kernel = functools.partial(assemble_kernel, slots)
    name = "assemble_units" if units else "assemble_attention"
    return kernel_call(kernel, name, arrays, [(shape, bf16)], blocks=blocks * 2)[0]


def place_kernel(chip_ref, rows_ref, out_ref):
    for index in range(16):
        rows = rows_ref[chip_ref[0] ^ int(MASKS[index])]
        place = slice(48 * index, 48 * index + 48)
        if len(out_ref.shape) == 2:
            out_ref[place] = rows
        else:
            for j in range(4):
                out_ref[j, place] = rows[:, 768 * j : 768 * j + 768]


def place_blocks(where, rows, units):
    shape = (4, 768, 768) if units else (768, 1664)
    name = "place_units" if units else "place_attention"
    return kernel_call(place_kernel, name, [where, rows], [(shape, bf16)], scalar=True)[0]


def pack_kernel(*refs):
    w_query, w_key, w_value, w_out, w_up, w_down, b_query, b_value = refs[:8]
    b_up = refs[9]
    vectors = [refs[8], *refs[10:15]]
    out_ref, vec_ref, small_ref = refs[15:]
    vec_ref[...] = jnp.zeros_like(vec_ref)
    for i, vector in enumerate(vectors):
        vec_ref[i : i + 1, 0:24] = vector[...].astype(f32)
    cols = vec_ref[...].T[0:24, 0:8]
    for half in range(2):
        small_ref[...] = jnp.zeros_like(small_ref)
        small_ref[:, 0:8] = cols
        small_ref[0:2, 8:11] = b_query[0, :, 3 * half : 3 * half + 3].astype(f32)
        small_ref[0:2, 11:14] = b_value[0, :, 3 * half : 3 * half + 3].astype(f32)
        small_ref[0:2, 14:26] = b_up[0, :, 12 * half : 12 * half + 12].astype(f32)
        small = small_ref[...].astype(bf16)
        wide, whole = slice(768 * half, 768 * half + 768), slice(192 * half, 192 * half + 192)
        first = jnp.concatenate([w_query[0, :, whole].astype(f32), w_key[0, :, whole].astype(f32)], 1).astype(bf16)
        second = jnp.concatenate([w_value[0, :, whole].astype(f32), w_out[0, :, whole].astype(f32)], 1).astype(bf16)
        for k in range(4):
            out = out_ref.at[2 * k + half]
            out[:, 0:768] = w_up[0, :, wide]
            out[:, 768:1536] = w_down[0, :, wide]
            out[:, 1536:1920] = first
            out[:, 1920:2304] = second
            out[:, 2304:2368] = small


def gather_start(params):
    tensor = lax.axis_index("tensor")
    rows = kernel_call(
        pack_kernel, "pack", list(params), [((8, 24, 2368), bf16)],
        scratch=[pltpu.VMEM((8, 128), f32), pltpu.VMEM((24, 64), f32)],
        blocks=[(param.shape, (0,) * param.ndim) for param in params], large=False,
    )[0]
    rows = lax.all_to_all(rows, ("pipe", "tensor", "core"), 0, 0, tiled=True)
    rows = rows.reshape(2, 2, 48, 2368)
    a = jnp.where(tensor == 0, rows[:, 0], rows[:, 1])
    b = jnp.where(tensor == 0, rows[:, 1], rows[:, 0])
    both = jnp.stack([a, b])
    one = both[:, 1]
    pieces = [one[t, :, 1536 + 192 * i : 1728 + 192 * i] for i in range(4) for t in range(2)]
    attn = jnp.concatenate(pieces + [one[0, :, 2304:], one[1, :, 2304:]], -1)
    units = jnp.concatenate([one[0, :, :768], one[1, :, :768], one[0, :, 768:1536], one[1, :, 768:1536]], -1)
    second = [lax.all_gather(group, ("z", "x"), axis=0) for group in (attn, units)]
    a, b = both[0, 0], both[1, 0]
    parts = [
        [a[:, 1536:1728], b[:, 1536:1728], a[:, :768]],
        [a[:, 1728:1920], b[:, 1728:1920], b[:, :768]],
        [a[:, 1920:2112], b[:, 1920:2112], a[:, 768:1536]],
        [a[:, 2112:2304], b[:, 2112:2304], a[:, 2304:], b[:, 2304:], b[:, 768:1536]],
    ]
    parts = [jnp.concatenate(part, -1)[None] for part in parts]
    for step in range(3):
        got = [exchange(part, ORDERS[i][step]) for i, part in enumerate(parts)]
        parts = [jnp.concatenate([x, y], 0) for x, y in zip(parts, got)]
    return parts, second


def gather_fourth(held):
    return [exchange(part, ORDERS[i][3]) for i, part in enumerate(held)]


def fold_kernel(fixed, outputs, *refs):
    terms, outs = refs[: len(fixed)], refs[len(fixed) :]
    for out, places in zip(outs, outputs):
        for sources, layer, start in places:
            total = None
            for term, index, first, width in sources:
                value = terms[term][(*index, *(0,) * fixed[term], slice(None), slice(None), slice(first, first + width))]
                total = value.astype(f32) if total is None else total + value.astype(f32)
            cols = slice(start, start + total.shape[-1])
            if layer is None:
                out[:, :, cols] = total.astype(bf16)
            else:
                out[layer, :, :, cols] = total.astype(bf16)


def fold(terms, outputs, layers, grid, name):
    arrays, specs, shapes, out_specs = [], [], [], []
    for array, bits in terms:
        lead, (n, rows, cols) = array.shape[:-3], array.shape[-3:]
        n >>= len(bits)
        arrays.append(array.reshape(*lead, *(2,) * len(bits), n, rows, cols))
        block = (*lead, *(1,) * len(bits), n // grid, rows, cols)
        specs.append(pl.BlockSpec(block, lambda b, at=(0,) * len(lead) + tuple(bits): (*at, b, 0, 0)))
    for places in outputs:
        width = max(start + sources[0][3] for sources, _, start in places)
        lead = () if layers is None else (layers,)
        shapes.append(jax.ShapeDtypeStruct((*lead, n, 48, width), bf16))
        out_specs.append(pl.BlockSpec((*lead, n // grid, 48, width), lambda b, at=(0,) * len(lead): (*at, b, 0, 0)))
    return pl.pallas_call(
        functools.partial(fold_kernel, [len(bits) for _, bits in terms], outputs),
        name=name,
        grid=(grid,),
        out_shape=shapes,
        in_specs=specs,
        out_specs=out_specs,
        cost_estimate=pl.CostEstimate(flops=1, bytes_accessed=1, transcendentals=0),
        compiler_params=pltpu.CompilerParams(vmem_limit_bytes=52 * 2**20),
    )(*arrays)


def send_parts(parts, step):
    return [exchange(part, ORDERS[i][step]) for i, part in enumerate(parts)]


def fold_attention(own, got):
    outputs = [[([(k, (), 384 * i, ATTN_COLS[i]) for k in range(2)], None, 0)] for i in range(4)]
    return fold([(own, (1,)), (got, (1,))], outputs, None, 2, "fold_attention")


def fold_units(own, got):
    outputs = [[([(k, (i,), 0, 768) for k in range(2)], None, 0)] for i in range(4)]
    return fold([(own, (1,)), (got, (1,))], outputs, None, 2, "fold_units")


def fold_both(groups, side):
    terms = []
    outputs = [[] for _ in range(4)]
    for units, (own, got, received) in enumerate(groups):
        base = len(terms)
        terms += [(own, (0, side)), (got, (0, side))] + [(part, (side,)) for part in received]
        for i in range(4):
            width = 768 if units else ATTN_COLS[i]
            index, first = ((i,), 0) if units else ((), 384 * i)
            sources = [(base, index, first, width), (base + 1, index, first, width), (base + 2 + i, (), 0, width)]
            outputs[i].append((sources, None, ATTN_COLS[i] * units))
    return fold(terms, outputs, None, 2, ("fold_both_kept", "fold_both_sent")[side])


def fold_on(kept, got, side, name):
    terms = [(part, (side,)) for pair in zip(kept, got) for part in pair]
    outputs = []
    for i in range(4):
        width = kept[i].shape[-1]
        outputs.append([([(2 * i + k, (), 0, width) for k in range(2)], None, 0)])
    return fold(terms, outputs, None, 1, name + ("_kept", "_sent")[side])


def collect_kernel(tensor_ref, *refs):
    kept, got, attn, units, out_ref = refs[:4], refs[4:8], refs[8], refs[9], refs[10]
    p = [x[0].astype(f32) + y[0].astype(f32) for x, y in zip(kept, got)]
    first = [part[:, : ATTN_COLS[i]] for i, part in enumerate(p)]
    wide = [part[:, ATTN_COLS[i] :] for i, part in enumerate(p)]
    layers = [
        (first, wide),
        (
            [attn[0, :, 384 * i : 384 * i + ATTN_COLS[i]].astype(f32) for i in range(4)],
            [units[0, :, 768 * i : 768 * i + 768].astype(f32) for i in range(4)],
        ),
    ]
    for layer, (first, wide) in enumerate(layers):
        for t in range(2):
            at = slice(192 * t, 192 * t + 192)
            values = [
                (0, wide[t]),
                (768, wide[2 + t]),
                (1536, jnp.concatenate([first[0][:, at], first[1][:, at]], 1)),
                (1920, jnp.concatenate([first[2][:, at], first[3][:, at]], 1)),
                (2304, first[3][:, 384 + 64 * t : 448 + 64 * t]),
            ]
            place = 4 * layer + 2 * (t ^ tensor_ref[0])
            for core in range(2):
                out = out_ref.at[place + core]
                for start, value in values:
                    out[:, start : start + value.shape[1]] = value[24 * core : 24 * core + 24].astype(bf16)


def finish_kernel(rows_ref, *refs):
    g_query, g_key, g_value, g_out, g_up, g_down, gb_query, gb_value = refs[:8]
    gb_up = refs[9]
    vectors = [refs[8], *refs[10:15]]
    small_ref = refs[15]
    halves = []
    for core in range(2):
        total = rows_ref[core].astype(f32)
        for k in range(1, 4):
            total = total + rows_ref[2 * k + core].astype(f32)
        halves.append(total)
        g_up[0, :, 768 * core : 768 * core + 768] = total[:, 0:768]
        g_down[0, :, 768 * core : 768 * core + 768] = total[:, 768:1536]
    for i, out in enumerate((g_query, g_key, g_value, g_out)):
        start = 1536 + 192 * i
        out[0] = jnp.concatenate([half[:, start : start + 192] for half in halves], 1)
    for out, lo, hi in ((gb_query, 8, 11), (gb_value, 11, 14), (gb_up, 14, 26)):
        out[0] = jnp.concatenate([half[0:2, 2304 + lo : 2304 + hi] for half in halves], 1)
    small_ref[...] = jnp.zeros_like(small_ref)
    small_ref[0:24, 0:64] = halves[0][:, 2304:2368]
    cols = small_ref[...].T
    for i, out in enumerate(vectors):
        out[...] = cols[i : i + 1, 0:24]


def scatter_end(kept, got, second):
    tensor = lax.axis_index("tensor").astype(jnp.int32).reshape(1)
    rows = kernel_call(collect_kernel, "collect", [tensor, *kept, *got, *second], [((8, 24, 2368), bf16)], scalar=True)[0]
    rows = lax.all_to_all(rows, ("pipe", "tensor", "core"), 0, 0, tiled=True)
    shapes = [(1, 24, 384)] * 4 + [(1, 24, 1536)] * 2 + [(1, 2, 6)] * 2 + [(1, 24), (1, 2, 24)] + [(1, 24)] * 5
    return kernel_call(
        finish_kernel, "finish", [rows], [(shape, f32) for shape in shapes], scratch=[pltpu.VMEM((128, 128), f32)]
    )


def share_outputs(first_rows, second_rows):
    pipe, tensor = lax.axis_index("pipe"), lax.axis_index("tensor")
    keep = jnp.where(pipe == 0, first_rows, second_rows)
    send = jnp.where(pipe == 0, second_rows, first_rows)
    return keep, exchange_tensor(keep), exchange_pipe(send), exchange_both(send)


def order_outputs(rows):
    pipe, tensor = lax.axis_index("pipe"), lax.axis_index("tensor")
    a, b, c, d = rows
    a, b = jnp.where(tensor == 0, a, b), jnp.where(tensor == 0, b, a)
    c, d = jnp.where(tensor == 0, c, d), jnp.where(tensor == 0, d, c)
    a, c = jnp.where(pipe == 0, a, c), jnp.where(pipe == 0, c, a)
    b, d = jnp.where(pipe == 0, b, d), jnp.where(pipe == 0, d, b)
    return jnp.stack([a, b, c, d])[None]


def local(clip_frames, out_cotangent, clip_lengths, *params):
    micro = lax.axis_index("pipe") * 2 + lax.axis_index("tensor")
    chip = lax.axis_index("z") * 4 + lax.axis_index("x")

    where = jnp.stack([chip, lax.axis_index("core")]).astype(jnp.int32)

    held, second = gather_start(params)
    got = gather_fourth(held)

    blocks = (chip ^ jnp.asarray(MASKS))[:, None]
    rows_at = (blocks * 48 + jnp.arange(48)[None]).reshape(-1)
    place_rows = (jnp.arange(768)[:, None] == rows_at[None]).astype(bf16)
    within = np.arange(48)
    units_at = np.where(within % 24 < 2, within // 24 * 2 + within % 24, 1000)
    units_at = (blocks * 4 + jnp.asarray(units_at)[None]).reshape(-1)
    place_units = (jnp.arange(64)[:, None] == units_at[None]).astype(bf16)
    place_back = (units_at[:, None] == jnp.arange(64)[None]).astype(bf16)

    frames = lax.dynamic_index_in_dim(clip_frames, micro, 0, keepdims=False)
    cotangent = lax.dynamic_index_in_dim(out_cotangent, micro, 0, keepdims=False)
    length = lax.dynamic_index_in_dim(clip_lengths, micro, 0, keepdims=False)
    x_first = dot(frames, place_rows).astype(bf16)
    grad_out = dot(cotangent, place_rows).astype(bf16)

    def placed_back(rows):
        return dot_cols(rows, place_rows).astype(bf16)

    attn_own = assemble(held, got, False)
    attn_own, got = pin(attn_own, got)
    attn_peer = exchange(attn_own, "c")
    units_own = assemble(held, got, True)
    attn_peer, units_own = pin(attn_peer, units_own)
    attn_first = attn_own, attn_peer
    units_first = units_own, exchange(units_own, "c")
    middle_first, heads_first, soft_first, mixed_first, vec_first, up_bias_first = attention_forward(
        length, x_first, attn_first, place_units
    )
    x_second, active_first, slope_first = units_forward(middle_first, units_first, vec_first, up_bias_first)
    x_second, second = pin(x_second, second)
    attn_own = place_blocks(where, second[0], False)
    attn_own, units_rows = pin(attn_own, second[1])
    attn_peer = exchange(attn_own, "c")
    units_own = place_blocks(where, units_rows, True)
    attn_peer, units_own = pin(attn_peer, units_own)
    attn_second = attn_own, attn_peer
    units_second = units_own, exchange(units_own, "c")
    middle_second, heads_second, soft_second, mixed_second, vec_second, up_bias_second = attention_forward(
        length, x_second, attn_second, place_units
    )
    out_second, active_second, slope_second = units_forward(middle_second, units_second, vec_second, up_bias_second)
    shared = share_outputs(placed_back(x_second), placed_back(out_second))

    shards = ("z", "x", "core")
    grad_middle, units_vec, up_bias_grad, units_placed = units_backward(
        grad_out, middle_second, active_second, slope_second, units_second, vec_second, where
    )
    units_total = lax.psum_scatter(units_placed, shards, scatter_dimension=0, tiled=True)
    second_grad, attn_placed = attention_backward(
        grad_middle, x_second, heads_second, soft_second, mixed_second, attn_second, vec_second, units_vec,
        up_bias_grad, place_back, where,
    )
    second_grad, attn_placed, shared = pin(second_grad, attn_placed, shared)
    attn_total = lax.psum_scatter(attn_placed, shards, scatter_dimension=0, tiled=True)
    section_output = order_outputs(shared)

    grad_middle, units_vec, up_bias_grad, units_own, units_peer = units_backward(
        second_grad, middle_first, active_first, slope_first, units_first, vec_first
    )
    units_got = exchange(units_peer, "c")
    attn = attention_backward(
        grad_middle, x_first, heads_first, soft_first, mixed_first, attn_first, vec_first, units_vec,
        up_bias_grad, place_back,
    )
    attn, units_got = pin(attn, units_got)
    first_grad, attn_own, attn_peer = attn
    units_fourth = send_parts(fold_units(units_own, units_got), 3)
    attn_got = exchange(attn_peer, "c")
    attn_fourth = send_parts(fold_attention(attn_own, attn_got), 3)
    input_grad = order_outputs(share_outputs(placed_back(first_grad), placed_back(second_grad)))

    groups = ((attn_own, attn_got, attn_fourth), (units_own, units_got, units_fourth))
    kept, got = fold_both(groups, 0), send_parts(fold_both(groups, 1), 2)
    kept, got = fold_on(kept, got, 0, "fold_four"), send_parts(fold_on(kept, got, 1, "fold_four"), 1)
    kept, got = fold_on(kept, got, 0, "fold_two"), send_parts(fold_on(kept, got, 1, "fold_two"), 0)
    return (section_output, input_grad, *scatter_end(kept, got, (attn_total, units_total)))


def solution(mesh):
    fine = Mesh(mesh.devices.reshape(2, 4, 4, 2, 2), ("pipe", "z", "x", "core", "tensor"))
    shard = ("z", "x", "core")
    rows = P(None, shard, None)
    matrix = P("pipe", shard, "tensor")
    vector = P("pipe", shard)
    params = (matrix,) * 8 + (vector, matrix) + (vector,) * 5
    return jax.shard_map(
        local,
        mesh=fine,
        in_specs=(rows, rows, P(None, shard)) + params,
        out_specs=(P("pipe", None, shard, None),) * 2 + params,
        check_vma=False,
    )
```

profile of v0, /device:TPU:0, one launch (start us, length us, event | category | flops | bytes accessed | tf_op | source)
XLA Modules:
  0.0 425.6 jit_solution(3314134428930304443)
XLA Ops:
  9.4 4.6 %all-to-all-start = ((bf16[8,24,2368]{2,1,0:T(8,128)(2,1)}), bf16[8,24,2368]{2,1,0:T(8,128)(2,1)S(1)}, u32[]{:S(2)}, u32[]{:S(2)}) async-start(bf16[8,24,2368]{2,1,0:T(8,128)(2,1)} %pack.1), calls=%async_computation | async-start | bytes 1867776 | tf_op jit(solution)/shard_map/all_to_all | solution.py:420
  14.0 14.4 %all-to-all-done = bf16[8,24,2368]{2,1,0:T(8,128)(2,1)S(1)} async-done(((bf16[8,24,2368]{2,1,0:T(8,128)(2,1)}), bf16[8,24,2368]{2,1,0:T(8,128)(2,1)S(1)}, u32[]{:S(2)}, u32[]{:S(2)}) %all-to-all-start) | async-done | bytes 909344 | tf_op jit(solution)/shard_map/all_to_all | solution.py:420
  43.9 3.6 collective-permute-done.1
  49.5 4.4 %collective-permute-start.8 = (bf16[4,48,1152]{2,1,0:T(8,128)(2,1)S(1)}, bf16[4,48,1152]{2,1,0:T(8,128)(2,1)S(1)}, u32[]{:S(2)}, u32[]{:S(2)}) collective-permute-start(bf16[4,48,1152]{2,1,0:T(8,128)(2,1)S(1)} %pad_maximum_fusion.8), channel_id=1, source_target_pairs={{0,4},{4,0},{8,12},{12,8},{1,5},{5,1},{9,13},{13,9},{2,6},{6,2},{1... | collective-permute-start | bytes 1327112 | tf_op jit(solution)/shard_map/ppermute | solution.py:319
  61.8 3.6 collective-permute-done.11
  65.8 3.8 collective-permute-start.14
  69.5 19.3 %collective-permute-done.12.refs_4_.refs_9_.refs_10_ = bf16[8,48,1152]{2,1,0:T(8,128)(2,1)S(1)} collective-permute-done((bf16[8,48,1152]{2,1,0:T(8,128)(2,1)S(1)}, bf16[8,48,1152]{2,1,0:T(8,128)(2,1)S(1)}, u32[]{:S(2)}, u32[]{:S(2)}) %collective-permute-start.12) | collective-permute-done | bytes 884768 | tf_op jit(solution)/shard_map/ppermute | solution.py:319
  88.9 4.5 %collective-permute-done.14.refs_6_.refs_13_.refs_14_ = bf16[8,48,1152]{2,1,0:T(8,128)(2,1)S(1)} collective-permute-done((bf16[8,48,1152]{2,1,0:T(8,128)(2,1)S(1)}, bf16[8,48,1152]{2,1,0:T(8,128)(2,1)S(1)}, u32[]{:S(2)}, u32[]{:S(2)}) %collective-permute-start.14) | collective-permute-done | bytes 884768 | tf_op jit(solution)/shard_map/ppermute | solution.py:319
  98.5 4.6 %assemble_units.1.own_ref.refs_4_ = bf16[4,768,768]{2,1,0:T(8,128)(2,1)} custom-call(bf16[8,48,1152]{2,1,0:T(8,128)(2,1)S(1)} %pad_maximum_fusion.1.refs_0_.refs_1_, bf16[8,48,1152]{2,1,0:T(8,128)(2,1)S(1)} %pad_maximum_fusion.1.refs_0_.refs_1_, bf16[8,48,1152]{2,1,0:T(8,128)(2,1)S(1)} %pad_maximum_fusion.2.refs_1_.refs_2_.refs_3_, ...), custom_call_target="tpu_custom_call" | custom-call | flops 1 | bytes 1 | tf_op jit(solution)/shard_map/assemble_units/pallas_call | solution.py:249
  105.5 8.6 %attention_forward.2 = (f32[192,768]{1,0:T(8,128)S(1)}, bf16[3,192,768]{2,1,0:T(8,128)(2,1)}, f32[12,192,192]{2,1,0:T(8,128)}, bf16[192,768]{1,0:T(8,128)(2,1)S(...) custom-call(s32[1]{0:T(128)} %bitcast.3.length_ref, bf16[192,768]{1,0:T(8,128)(2,1)S(1)} %fusion.7.x_ref.refs_1_, ...), custom_call_target="tpu_custom_call" | custom-call | flops 1 | bytes 1 | tf_op jit(solution)/shard_map/attention_forward/pallas_call | solution.py:249
  114.1 8.1 %units_forward.2 = (bf16[192,768]{1,0:T(8,128)(2,1)S(1)}, bf16[192,3072]{1,0:T(8,128)(2,1)}, f32[192,3072]{1,0:T(8,128)}) custom-call(f32[192,768]{1,0:T(8,128)S(1)} %get-tuple-element.126.middle_ref.refs_1_, bf16[4,768,768]{2,1,0:T(8,128)(2,1)} %assemble_units.1.own_ref.refs_4_, bf16[4,768,768]{2,1,0:T(8,128)(2,1)} %collective-permute-done.17.peer_ref.refs_5_, ...), custom_call_target="tpu_custom_call" | custom-call | flops 1 | bytes 1 | tf_op jit(solution)/shard_map/units_forward/pallas_call | solution.py:249
  122.2 20.0 %all-gather.7.cloned.1.call-done = bf16[768,3072]{1,0:T(8,128)(2,1)} async-done(((bf16[48,3072]{1,0:T(8,128)(2,1)}), bf16[768,3072]{1,0:T(8,128)(2,1)}) %all-gather.7.cloned.1.call-update) | async-done | bytes 4718608 | tf_op jit(solution)/shard_map/all_gather | solution.py:429
  145.6 4.9 %place_units.1.own_ref.refs_5_ = bf16[4,768,768]{2,1,0:T(8,128)(2,1)} custom-call(s32[2]{0:T(128)S(1)} %pad_add_fusion.chip_ref.refs_0_, bf16[16,48,3072]{2,1,0:T(8,128)(2,1)} %bitcast.158), custom_call_target="tpu_custom_call" | custom-call | flops 1 | bytes 1 | tf_op jit(solution)/shard_map/place_units/pallas_call | solution.py:249
  151.8 8.6 %attention_forward.3 = (f32[192,768]{1,0:T(8,128)S(1)}, bf16[3,192,768]{2,1,0:T(8,128)(2,1)}, f32[12,192,192]{2,1,0:T(8,128)}, bf16[192,768]{1,0:T(8,128)(2,1)S(...) custom-call(s32[1]{0:T(128)} %bitcast.3.length_ref, bf16[192,768]{1,0:T(8,128)(2,1)S(1)} %get-tuple-element.131.x_ref.refs_2_, ...), custom_call_target="tpu_custom_call" | custom-call | flops 1 | bytes 1 | tf_op jit(solution)/shard_map/attention_forward/pallas_call | solution.py:249
  160.3 8.1 %units_forward.3 = (bf16[192,768]{1,0:T(8,128)(2,1)S(1)}, bf16[192,3072]{1,0:T(8,128)(2,1)}, f32[192,3072]{1,0:T(8,128)}) custom-call(f32[192,768]{1,0:T(8,128)S(1)} %get-tuple-element.137.middle_ref.refs_2_, bf16[4,768,768]{2,1,0:T(8,128)(2,1)} %place_units.1.own_ref.refs_5_, bf16[4,768,768]{2,1,0:T(8,128)(2,1)} %collective-permute-done.19.peer_ref.refs_6_, ...), custom_call_target="tpu_custom_call" | custom-call | flops 1 | bytes 1 | tf_op jit(solution)/shard_map/units_forward/pallas_call | solution.py:249
  175.6 13.3 %units_backward.2 = (f32[192,768]{1,0:T(8,128)S(1)}, f32[8,768]{1,0:T(8,128)S(1)}, f32[1,3072]{1,0:T(1,128)S(1)}, bf16[32,48,3072]{2,1,0:T(8,128)(2,1)}) custom-call(s32[2]{0:T(128)S(1)} %pad_add_fusion.chip_ref.refs_0_, bf16[192,768]{1,0:T(8,128)(2,1)S(1)} %fusion.6.refs_1_, f32[192,768]{1,0:T(8,128)S(1)} %get-tuple-element.137.middle_ref.refs_2_, ...), custom_call_target="tpu_custom_call" | custom-call | flops 1 | bytes 1 | tf_op jit(solution)/shard_map/units_backward/pallas_call | solution.py:249
  189.0 14.0 %attention_backward.2 = (bf16[192,768]{1,0:T(8,128)(2,1)S(1)}, bf16[32,48,1664]{2,1,0:T(8,128)(2,1)}) custom-call(s32[2]{0:T(128)S(1)} %pad_add_fusion.chip_ref.refs_0_, f32[192,768]{1,0:T(8,128)S(1)} %get-tuple-element.143.refs_1_, bf16[192,768]{1,0:T(8,128)(2,1)S(1)} %get-tuple-element.131.x_ref.refs_2_, bf16[3,192,768]{2,1,0:T(8,128)(2,1)} %get-tuple-element.144.refs_3_, ...), custom_call_target="tpu_custom_call" | custom-call | flops 1 | bytes 1 | tf_op jit(solution)/shard_map/attention_backward/pallas_call | solution.py:249
  203.6 11.6 %units_backward.3 = (f32[192,768]{1,0:T(8,128)S(1)}, f32[8,768]{1,0:T(8,128)S(1)}, f32[1,3072]{1,0:T(1,128)S(1)}, bf16[4,16,48,768]{3,2,1,0:T(8,128)(2,1)}, bf16[4,16,48,768]{3,2,1,0:T(8,128)(2,1)}) custom-call(bf16[192,768]{1,0:T(8,128)(2,1)S(1)} %get-tuple-element.156.refs_0_, f32[192,768]{1,0:T(8,128)S(1)} %get-tuple-element.126.middle_ref.refs_1_, ...), custom_call_target="tpu_custom_call" | custom-call | flops 1 | bytes 1 | tf_op jit(solution)/shard_map/units_backward/pallas_call | solution.py:249
  215.3 14.0 %attention_backward.3 = (bf16[192,768]{1,0:T(8,128)(2,1)S(1)}, bf16[16,48,1664]{2,1,0:T(8,128)(2,1)}, bf16[16,48,1664]{2,1,0:T(8,128)(2,1)}) custom-call(f32[192,768]{1,0:T(8,128)S(1)} %get-tuple-element.159.refs_0_, bf16[192,768]{1,0:T(8,128)(2,1)S(1)} %fusion.7.x_ref.refs_1_, bf16[3,192,768]{2,1,0:T(8,128)(2,1)} %get-tuple-element.160.refs_2_, ...), custom_call_target="tpu_custom_call" | custom-call | flops 1 | bytes 1 | tf_op jit(solution)/shard_map/attention_backward/pallas_call | solution.py:249
  242.9 8.8 %collective-permute-done.32 = bf16[8,48,768]{2,1,0:T(8,128)(2,1)S(1)} collective-permute-done((bf16[8,48,768]{2,1,0:T(8,128)(2,1)S(1)}, bf16[8,48,768]{2,1,0:T(8,128)(2,1)S(1)}, u32[]{:S(2)}, u32[]{:S(2)}) %collective-permute-start.32) | collective-permute-done | bytes 589856 | tf_op jit(solution)/shard_map/ppermute | solution.py:319
  255.4 9.0 %collective-permute-done.28 = bf16[8,48,384]{2,1,0:T(8,128)(2,1)S(1)} collective-permute-done((bf16[8,48,384]{2,1,0:T(8,128)(2,1)S(1)}, bf16[8,48,384]{2,1,0:T(8,128)(2,1)S(1)}, u32[]{:S(2)}, u32[]{:S(2)}) %collective-permute-start.28) | collective-permute-done | bytes 294944 | tf_op jit(solution)/shard_map/ppermute | solution.py:319
  313.3 82.9 %reduce-scatter.5.cloned.1.call-done.refs_9_ = bf16[1,48,3072]{2,1,0:T(8,128)(2,1)} async-done(((bf16[32,48,3072]{2,1,0:T(8,128)(2,1)}), bf16[1,48,3072]{2,1,0:T(8,128)(2,1)}) %reduce-scatter.5.cloned.1.call-update) | async-done | bytes 294928 | tf_op jit(solution)/shard_map/reduce_scatter | solution.py:662
  399.2 4.3 %all-to-all-start.1 = ((bf16[8,24,2368]{2,1,0:T(8,128)(2,1)}), bf16[8,24,2368]{2,1,0:T(8,128)(2,1)S(1)}, u32[]{:S(2)}, u32[]{:S(2)}) async-start(bf16[8,24,2368]{2,1,0:T(8,128)(2,1)} %collect.1), calls=%async_computation.3 | async-start | bytes 1867776 | tf_op jit(solution)/shard_map/all_to_all | solution.py:582
  407.3 10.7 %all-to-all-done.1.rows_ref = bf16[8,24,2368]{2,1,0:T(8,128)(2,1)S(1)} async-done(((bf16[8,24,2368]{2,1,0:T(8,128)(2,1)}), bf16[8,24,2368]{2,1,0:T(8,128)(2,1)S(1)}, u32[]{:S(2)}, u32[]{:S(2)}) %all-to-all-start.1) | async-done | bytes 909344 | tf_op jit(solution)/shard_map/all_to_all | solution.py:582
  (203 shorter events, 121.4 us)
Async XLA Ops:
  9.4 19.0 %all-to-all-start = ((bf16[8,24,2368]{2,1,0:T(8,128)(2,1)}), bf16[8,24,2368]{2,1,0:T(8,128)(2,1)S(1)}, u32[]{:S(2)}, u32[]{:S(2)}) async-start(bf16[8,24,2368]{2,1,0:T(8,128)(2,1)} %pack.1), calls=%async_computation | async-start | bytes 1867776 | tf_op jit(solution)/shard_map/all_to_all | solution.py:420
  14.0 108.2 %all-gather.5.cloned.1.call-start = ((), (), s32[]{:S(2)}) async-start(), calls=%async_computation.6 | async-start | bytes 2715648 | tf_op jit(solution)/shard_map/all_gather | solution.py:429
  29.5 112.7 %all-gather.7.cloned.1.call-start = ((), (), s32[]{:S(2)}) async-start(), calls=%async_computation.7 | async-start | bytes 5013504 | tf_op jit(solution)/shard_map/all_gather | solution.py:429
  39.4 274.0 %reduce-scatter.3.cloned.1.call-start = ((), (), s32[]{:S(2)}) async-start(), calls=%async_computation.4 | async-start | bytes 5271552 | tf_op jit(solution)/shard_map/reduce_scatter | solution.py:668
  49.5 16.1 %collective-permute-start.8 = (bf16[4,48,1152]{2,1,0:T(8,128)(2,1)S(1)}, bf16[4,48,1152]{2,1,0:T(8,128)(2,1)S(1)}, u32[]{:S(2)}, u32[]{:S(2)}) collective-permute-start(bf16[4,48,1152]{2,1,0:T(8,128)(2,1)S(1)} %pad_maximum_fusion.8), channel_id=1, source_target_pairs={{0,4},{4,0},{8,12},{12,8},{1,5},{5,1},{9,13},{13,9},{2,6},{6,2},{1... | collective-permute-start | bytes 1327112 | tf_op jit(solution)/shard_map/ppermute | solution.py:319
  59.5 29.3 %collective-permute-start.12 = (bf16[8,48,1152]{2,1,0:T(8,128)(2,1)S(1)}, bf16[8,48,1152]{2,1,0:T(8,128)(2,1)S(1)}, u32[]{:S(2)}, u32[]{:S(2)}) collective-permute-start(bf16[8,48,1152]{2,1,0:T(8,128)(2,1)S(1)} %pad_maximum_fusion.1.refs_0_.refs_1_), channel_id=1, source_target_pairs={{0,48},{16,32},{32,16},{48,0},{1,49},{17,33},{33,17},{49,1},{2,50}... | collective-permute-start | bytes 2654216 | tf_op jit(solution)/shard_map/ppermute | solution.py:319
  61.7 27.1 %collective-permute-start.13 = (bf16[8,48,1152]{2,1,0:T(8,128)(2,1)S(1)}, bf16[8,48,1152]{2,1,0:T(8,128)(2,1)S(1)}, u32[]{:S(2)}, u32[]{:S(2)}) collective-permute-start(bf16[8,48,1152]{2,1,0:T(8,128)(2,1)S(1)} %pad_maximum_fusion.2.refs_1_.refs_2_.refs_3_), channel_id=1, source_target_pairs={{0,16},{16,0},{32,48},{48,32},{1,17},{17,1},{33,49},{49,33},{2,18}... | collective-permute-start | bytes 2654216 | tf_op jit(solution)/shard_map/ppermute | solution.py:319
  65.5 27.8 %collective-permute-start.15 = (bf16[8,48,1280]{2,1,0:T(8,128)(2,1)S(1)}, bf16[8,48,1280]{2,1,0:T(8,128)(2,1)S(1)}, u32[]{:S(2)}, u32[]{:S(2)}) collective-permute-start(bf16[8,48,1280]{2,1,0:T(8,128)(2,1)S(1)} %pad_maximum_fusion.refs_3_.refs_6_.refs_7_.refs_8_), channel_id=1, source_target_pairs={{0,4},{4,0},{8,12},{12,8},{1,5},{5,1},{9,13},{13,9},{2,6},{6,2},{1... | collective-permute-start | bytes 2949128 | tf_op jit(solution)/shard_map/ppermute | solution.py:319
  65.8 27.6 %collective-permute-start.14 = (bf16[8,48,1152]{2,1,0:T(8,128)(2,1)S(1)}, bf16[8,48,1152]{2,1,0:T(8,128)(2,1)S(1)}, u32[]{:S(2)}, u32[]{:S(2)}) collective-permute-start(bf16[8,48,1152]{2,1,0:T(8,128)(2,1)S(1)} %pad_maximum_fusion.3.refs_2_.refs_4_.refs_5_), channel_id=1, source_target_pairs={{0,12},{4,8},{8,4},{12,0},{1,13},{5,9},{9,5},{13,1},{2,14},{6,10},... | collective-permute-start | bytes 2654216 | tf_op jit(solution)/shard_map/ppermute | solution.py:319
  169.1 33.9 %collective-permute-start.21 = (bf16[192,768]{1,0:T(8,128)(2,1)S(1)}, bf16[192,768]{1,0:T(8,128)(2,1)S(1)}, u32[]{:S(2)}, u32[]{:S(2)}) collective-permute-start(bf16[192,768]{1,0:T(8,128)(2,1)S(1)} %get-tuple-element.235), channel_id=1, source_target_pairs={{0,64},{64,0},{1,65},{65,1},{2,66},{66,2},{3,67},{67,3},{4,68},{68... | collective-permute-start | bytes 884744 | tf_op jit(solution)/shard_map/ppermute | solution.py:323
  170.7 32.3 %collective-permute-start.22 = (bf16[192,768]{1,0:T(8,128)(2,1)S(1)}, bf16[192,768]{1,0:T(8,128)(2,1)S(1)}, u32[]{:S(2)}, u32[]{:S(2)}) collective-permute-start(bf16[192,768]{1,0:T(8,128)(2,1)S(1)} %get-tuple-element.235), channel_id=1, source_target_pairs={{0,65},{1,64},{64,1},{65,0},{2,67},{3,66},{66,3},{67,2},{4,69},{5,... | collective-permute-start | bytes 884744 | tf_op jit(solution)/shard_map/ppermute | solution.py:327
  172.8 30.2 %collective-permute-start.20 = (bf16[192,768]{1,0:T(8,128)(2,1)S(1)}, bf16[192,768]{1,0:T(8,128)(2,1)S(1)}, u32[]{:S(2)}, u32[]{:S(2)}) collective-permute-start(bf16[192,768]{1,0:T(8,128)(2,1)S(1)} %get-tuple-element.152), channel_id=1, source_target_pairs={{0,1},{1,0},{2,3},{3,2},{4,5},{5,4},{6,7},{7,6},{8,9},{9,8},{10,11... | collective-permute-start | bytes 884744 | tf_op jit(solution)/shard_map/ppermute | solution.py:331
  203.1 193.2 %reduce-scatter.5.cloned.1.call-start = ((), (), s32[]{:S(2)}) async-start(), calls=%async_computation.5 | async-start | bytes 9732096 | tf_op jit(solution)/shard_map/reduce_scatter | solution.py:662
  234.8 16.9 %collective-permute-start.32 = (bf16[8,48,768]{2,1,0:T(8,128)(2,1)S(1)}, bf16[8,48,768]{2,1,0:T(8,128)(2,1)S(1)}, u32[]{:S(2)}, u32[]{:S(2)}) collective-permute-start(bf16[8,48,768]{2,1,0:T(8,128)(2,1)S(1)} %get-tuple-element.178), channel_id=1, source_target_pairs={{0,48},{16,32},{32,16},{48,0},{1,49},{17,33},{33,17},{49,1},{2,50}... | collective-permute-start | bytes 1769480 | tf_op jit(solution)/shard_map/ppermute | solution.py:319
  237.5 16.8 %collective-permute-start.33 = (bf16[8,48,768]{2,1,0:T(8,128)(2,1)S(1)}, bf16[8,48,768]{2,1,0:T(8,128)(2,1)S(1)}, u32[]{:S(2)}, u32[]{:S(2)}) collective-permute-start(bf16[8,48,768]{2,1,0:T(8,128)(2,1)S(1)} %get-tuple-element.179), channel_id=1, source_target_pairs={{0,16},{16,0},{32,48},{48,32},{1,17},{17,1},{33,49},{49,33},{2,18}... | collective-permute-start | bytes 1769480 | tf_op jit(solution)/shard_map/ppermute | solution.py:319
  237.7 16.7 %collective-permute-start.34 = (bf16[8,48,768]{2,1,0:T(8,128)(2,1)S(1)}, bf16[8,48,768]{2,1,0:T(8,128)(2,1)S(1)}, u32[]{:S(2)}, u32[]{:S(2)}) collective-permute-start(bf16[8,48,768]{2,1,0:T(8,128)(2,1)S(1)} %get-tuple-element.180), channel_id=1, source_target_pairs={{0,12},{4,8},{8,4},{12,0},{1,13},{5,9},{9,5},{13,1},{2,14},{6,10},... | collective-permute-start | bytes 1769480 | tf_op jit(solution)/shard_map/ppermute | solution.py:319
  238.9 16.5 %collective-permute-start.35 = (bf16[8,48,768]{2,1,0:T(8,128)(2,1)}, bf16[8,48,768]{2,1,0:T(8,128)(2,1)S(1)}, u32[]{:S(2)}, u32[]{:S(2)}) collective-permute-start(bf16[8,48,768]{2,1,0:T(8,128)(2,1)} %get-tuple-element.181), channel_id=1, source_target_pairs={{0,4},{4,0},{8,12},{12,8},{1,5},{5,1},{9,13},{13,9},{2,6},{6,2},{1... | collective-permute-start | bytes 1769480 | tf_op jit(solution)/shard_map/ppermute | solution.py:319
  241.0 27.9 %collective-permute-start.31 = (bf16[8,48,512]{2,1,0:T(8,128)(2,1)S(1)}, bf16[8,48,512]{2,1,0:T(8,128)(2,1)S(1)}, u32[]{:S(2)}, u32[]{:S(2)}) collective-permute-start(bf16[8,48,512]{2,1,0:T(8,128)(2,1)S(1)} %get-tuple-element.175), channel_id=1, source_target_pairs={{0,4},{4,0},{8,12},{12,8},{1,5},{5,1},{9,13},{13,9},{2,6},{6,2},{1... | collective-permute-start | bytes 1179656 | tf_op jit(solution)/shard_map/ppermute | solution.py:319
  254.3 14.5 %collective-permute-start.30 = (bf16[8,48,384]{2,1,0:T(8,128)(2,1)S(1)}, bf16[8,48,384]{2,1,0:T(8,128)(2,1)S(1)}, u32[]{:S(2)}, u32[]{:S(2)}) collective-permute-start(bf16[8,48,384]{2,1,0:T(8,128)(2,1)S(1)} %get-tuple-element.174), channel_id=1, source_target_pairs={{0,12},{4,8},{8,4},{12,0},{1,13},{5,9},{9,5},{13,1},{2,14},{6,10},... | collective-permute-start | bytes 884744 | tf_op jit(solution)/shard_map/ppermute | solution.py:319
  272.4 15.5 %collective-permute-start.39 = (bf16[4,48,1280]{2,1,0:T(8,128)(2,1)}, bf16[4,48,1280]{2,1,0:T(8,128)(2,1)S(1)}, u32[]{:S(2)}, u32[]{:S(2)}) collective-permute-start(bf16[4,48,1280]{2,1,0:T(8,128)(2,1)} %get-tuple-element.189), channel_id=1, source_target_pairs={{0,12},{4,8},{8,4},{12,0},{1,13},{5,9},{9,5},{13,1},{2,14},{6,10},... | collective-permute-start | bytes 1474568 | tf_op jit(solution)/shard_map/ppermute | solution.py:319
  307.9 96.9 %collective-permute-start.25 = (bf16[192,768]{1,0:T(8,128)(2,1)}, bf16[192,768]{1,0:T(8,128)(2,1)}, u32[]{:S(2)}, u32[]{:S(2)}) collective-permute-start(bf16[192,768]{1,0:T(8,128)(2,1)} %get-tuple-element.233), channel_id=1, source_target_pairs={{0,64},{64,0},{1,65},{65,1},{2,66},{66,2},{3,67},{67,3},{4,68},{68... | collective-permute-start | bytes 884744 | tf_op jit(solution)/shard_map/ppermute | solution.py:323
  310.2 94.5 %collective-permute-start.26 = (bf16[192,768]{1,0:T(8,128)(2,1)}, bf16[192,768]{1,0:T(8,128)(2,1)}, u32[]{:S(2)}, u32[]{:S(2)}) collective-permute-start(bf16[192,768]{1,0:T(8,128)(2,1)} %get-tuple-element.233), channel_id=1, source_target_pairs={{0,65},{1,64},{64,1},{65,0},{2,67},{3,66},{66,3},{67,2},{4,69},{5,... | collective-permute-start | bytes 884744 | tf_op jit(solution)/shard_map/ppermute | solution.py:327
  312.3 92.5 %collective-permute-start.24 = (bf16[192,768]{1,0:T(8,128)(2,1)}, bf16[192,768]{1,0:T(8,128)(2,1)}, u32[]{:S(2)}, u32[]{:S(2)}) collective-permute-start(bf16[192,768]{1,0:T(8,128)(2,1)} %get-tuple-element.234), channel_id=1, source_target_pairs={{0,1},{1,0},{2,3},{3,2},{4,5},{5,4},{6,7},{7,6},{8,9},{9,8},{10,11... | collective-permute-start | bytes 884744 | tf_op jit(solution)/shard_map/ppermute | solution.py:331
  399.2 18.7 %all-to-all-start.1 = ((bf16[8,24,2368]{2,1,0:T(8,128)(2,1)}), bf16[8,24,2368]{2,1,0:T(8,128)(2,1)S(1)}, u32[]{:S(2)}, u32[]{:S(2)}) async-start(bf16[8,24,2368]{2,1,0:T(8,128)(2,1)} %collect.1), calls=%async_computation.3 | async-start | bytes 1867776 | tf_op jit(solution)/shard_map/all_to_all | solution.py:582
  (52 other events, 546.0 us)
Sparse Core Ops, SparseCore 0:
  29.6 56.0 all-gather.4
  87.8 54.3 all-gather.6
  203.2 94.8 reduce-scatter.2
  301.7 94.4 reduce-scatter.4
where the time goes:
time: 432 us; the launch traced here: 426 us
  waiting for transfers between devices  196 us (45%)
  Pallas kernels  124 us (29%)
  starting transfers between devices  70.7 us (16%)
  between operations  14.5 us (3%)
  local copies, waits for them, and re-layouts  9.24 us (2%)
  other arithmetic  5.75 us (1%)
  matrix products  5.59 us (1%)
    pallas_call x15, Pallas kernels, kernel_call(): pl.pallas_call(kernel, name=name, out_shape=shapes, in_specs=specs, out_s...  107 us
    reduce_scatter x1, waiting for transfers between devices, local(): lax.psum_scatter(units_placed, shards, scatter_dimension=0, tiled=True)  82.9 us
    ppermute x42, waiting for transfers between devices, exchange(): return lax.ppermute(value, axis, [(i, i ^ flip) for i in range(size)])  67.1 us
    ppermute x42, starting transfers between devices, exchange(): return lax.ppermute(value, axis, [(i, i ^ flip) for i in range(size)])  52.6 us
    all_gather x2, waiting for transfers between devices, gather_start(): lax.all_gather(group, ('z', 'x'), axis=0)  20 us
    pallas_call x8, Pallas kernels, fold(): pl.pallas_call(functools.partial(fold_kernel, [len(bits) for _, bits in t...  17.5 us
    all_to_all x1, waiting for transfers between devices, gather_start(): rows = lax.all_to_all(rows, ('pipe', 'tensor', 'core'), 0, 0, tiled=True)  14.4 us
    all_to_all x1, waiting for transfers between devices, scatter_end(): rows = lax.all_to_all(rows, ('pipe', 'tensor', 'core'), 0, 0, tiled=True)  10.7 us
  transfers between devices with their start and end apart: 54, of which 22 were waited for; matrix products, arithmetic and copies ran while one was open for 3% of the time, Pallas kernels for 26%

commit v1 on v0

--- a/solution.py
+++ b/solution.py
@@ -145,8 +145,8 @@
 def units_backward_kernel(placed, *refs):
     where_ref, refs = (refs[0], refs[1:]) if placed else (None, refs)
     grad_ref, middle_ref, active_ref, slope_ref, own_ref, peer_ref, vec_ref = refs[:7]
-    grad_middle_ref, vec_grad_ref, up_bias_grad_ref, grad_own_ref = refs[7:11]
-    grad_peer_ref = grad_own_ref if placed else refs[11]
+    grad_middle_ref, vec_grad_ref, up_bias_grad_ref = refs[7:10]
+    grad_own_ref, grad_peer_ref = (refs[11], refs[11]) if placed else refs[10:12]
     grad_b = grad_ref[...]
     grad_rows = grad_b.astype(f32)
     normed, rescale = norm_parts(middle_ref[...])
@@ -172,14 +172,19 @@
     vec_grad_ref[1:2] = jnp.sum(grad_rows, 0, keepdims=True)
     vec_grad_ref[4:5] = jnp.sum(grad_normed * normed, 0, keepdims=True)
     vec_grad_ref[5:6] = jnp.sum(grad_normed, 0, keepdims=True)
+    if placed:
+        copy = pltpu.make_async_copy(grad_own_ref, refs[10].at[:, :, pl.ds(1664, 3072)], refs[12])
+        copy.start()
+        copy.wait()
 
 
 def attention_backward_kernel(placed, *refs):
     where_ref, refs = (refs[0], refs[1:]) if placed else (None, refs)
     grad_ref, x_ref, heads_ref, soft_ref, mixed_ref, own_ref, peer_ref, vec_ref = refs[:8]
-    units_vec_ref, up_bias_grad_ref, place_ref, grad_in_ref, grad_own_ref = refs[8:13]
-    grad_peer_ref = grad_own_ref if placed else refs[13]
-    grad_mixed_ref, grad_heads_ref, cols_ref, small_ref = refs[-4:]
+    units_vec_ref, up_bias_grad_ref, place_ref = refs[8:11]
+    refs = refs[12:] if placed else refs[11:]
+    grad_in_ref, grad_mixed_ref, grad_heads_ref, cols_ref, small_ref = refs[0], *refs[-4:]
+    grad_own_ref, grad_peer_ref = (refs[2], refs[2]) if placed else refs[1:3]
     grad_b = grad_ref[...].astype(bf16)
     grad_t = grad_b.T
     grad_mixed_ref[:, :384] = dot(grad_b, own_ref[:, 1152:1536]).astype(bf16)
@@ -234,9 +239,13 @@
         small = dot_cols(place_ref[...], small_ref[...].astype(bf16)) + cols
         weight = dot(grad_t, mixed_ref[:, 384 * half : 384 * half + 384])
         put_blocks(out_ref, 3, half, None, 1152, jnp.concatenate([weight, small], 1), where_ref)
-
-
-def kernel_call(kernel, name, inputs, outputs, scratch=(), scalar=False, blocks=None, large=True):
+    if placed:
+        copy = pltpu.make_async_copy(grad_own_ref, refs[1].at[:, :, pl.ds(0, 1664)], refs[3])
+        copy.start()
+        copy.wait()
+
+
+def kernel_call(kernel, name, inputs, outputs, scratch=(), scalar=False, blocks=None, large=True, apart=None, aliases=None):
     whole = pl.BlockSpec(memory_space=pltpu.VMEM)
     specs = [whole] * len(inputs)
     out_specs = [whole] * len(outputs)
@@ -245,6 +254,10 @@
         out_specs = [pl.BlockSpec(shape, lambda i, n=len(shape): (0,) * n) for shape, _ in outputs]
     if scalar:
         specs[0] = pl.BlockSpec(memory_space=pltpu.SMEM)
+    if apart is not None:
+        out_specs[apart] = pl.BlockSpec(memory_space=pl.ANY)
+    for number in aliases or {}:
+        specs[number] = pl.BlockSpec(memory_space=pl.ANY)
     shapes = [jax.ShapeDtypeStruct(shape, dtype) for shape, dtype in outputs]
     return pl.pallas_call(
         kernel,
@@ -253,6 +266,7 @@
         in_specs=specs,
         out_specs=out_specs,
         grid=() if blocks is None else (1,),
+        input_output_aliases=aliases or {},
         scratch_shapes=list(scratch),
         cost_estimate=pl.CostEstimate(flops=1, bytes_accessed=1, transcendentals=0),
         compiler_params=pltpu.CompilerParams(vmem_limit_bytes=52 * 2**20 if large else None),
@@ -263,8 +277,7 @@
 HEADS_SHAPE = (3, 192, 768)
 UNITS_SHAPE = (4, 16, 48, 768)
 ATTN_SHAPE = (16, 48, 1664)
-PLACED_UNITS = (32, 48, 3072)
-PLACED_ATTN = (32, 48, 1664)
+PLACED_SHAPE = (32, 48, 4736)
 
 
 def attention_forward(length, x, attn, place_units):
@@ -288,29 +301,34 @@
 def units_backward(grad_b, middle, active, slope, units, vec, where=None):
     own, peer = units
     placed = where is not None
-    shapes = [PLACED_UNITS] if placed else [UNITS_SHAPE] * 2
+    shapes = [PLACED_SHAPE] if placed else [UNITS_SHAPE] * 2
     return kernel_call(
         functools.partial(units_backward_kernel, placed), "units_backward",
         [where] * placed + [grad_b, middle, active, slope, own, peer, vec],
         [(ROWS, f32), ((8, 768), f32), ((1, 3072), f32)] + [(shape, bf16) for shape in shapes], scalar=placed,
+        scratch=[pltpu.VMEM((32, 48, 3072), bf16), pltpu.SemaphoreType.DMA(())] * placed,
+        apart=3 if placed else None,
     )
 
 
 def attention_backward(
-    grad_middle, x, heads, soft, mixed, attn, vec, units_vec, up_bias_grad, place_units, where=None
+    grad_middle, x, heads, soft, mixed, attn, vec, units_vec, up_bias_grad, place_units, where=None, placed_units=None
 ):
     own, peer = attn
     placed = where is not None
-    shapes = [PLACED_ATTN] if placed else [ATTN_SHAPE] * 2
+    shapes = [PLACED_SHAPE] if placed else [ATTN_SHAPE] * 2
     return kernel_call(
         functools.partial(attention_backward_kernel, placed), "attention_backward",
         [where] * placed
-        + [grad_middle, x, heads, soft, mixed, own, peer, vec, units_vec, up_bias_grad, place_units],
+        + [grad_middle, x, heads, soft, mixed, own, peer, vec, units_vec, up_bias_grad, place_units]
+        + [placed_units] * placed,
         [(ROWS, bf16)] + [(shape, bf16) for shape in shapes], scalar=placed,
-        scratch=[
+        scratch=[pltpu.VMEM((32, 48, 1664), bf16), pltpu.SemaphoreType.DMA(())] * placed
+        + [
             pltpu.VMEM(ROWS, bf16), pltpu.VMEM(HEADS_SHAPE, bf16), pltpu.VMEM((128, 768), f32),
             pltpu.VMEM((128, 64), f32),
         ],
+        apart=1 if placed else None, aliases={12: 1} if placed else None,
     )
 
 
@@ -367,13 +385,13 @@
 
 def place_kernel(chip_ref, rows_ref, out_ref):
     for index in range(16):
-        rows = rows_ref[chip_ref[0] ^ int(MASKS[index])]
+        block = rows_ref.at[chip_ref[0] ^ int(MASKS[index])]
         place = slice(48 * index, 48 * index + 48)
         if len(out_ref.shape) == 2:
-            out_ref[place] = rows
+            out_ref[place] = block[:, :1664]
         else:
             for j in range(4):
-                out_ref[j, place] = rows[:, 768 * j : 768 * j + 768]
+                out_ref[j, place] = block[:, 1664 + 768 * j : 2432 + 768 * j]
 
 
 def place_blocks(where, rows, units):
@@ -424,9 +442,9 @@
     both = jnp.stack([a, b])
     one = both[:, 1]
     pieces = [one[t, :, 1536 + 192 * i : 1728 + 192 * i] for i in range(4) for t in range(2)]
-    attn = jnp.concatenate(pieces + [one[0, :, 2304:], one[1, :, 2304:]], -1)
-    units = jnp.concatenate([one[0, :, :768], one[1, :, :768], one[0, :, 768:1536], one[1, :, 768:1536]], -1)
-    second = [lax.all_gather(group, ("z", "x"), axis=0) for group in (attn, units)]
+    pieces += [one[0, :, 2304:], one[1, :, 2304:]]
+    pieces += [one[0, :, :768], one[1, :, :768], one[0, :, 768:1536], one[1, :, 768:1536]]
+    second = lax.all_gather(jnp.concatenate(pieces, -1), ("z", "x"), axis=0)
     a, b = both[0, 0], both[1, 0]
     parts = [
         [a[:, 1536:1728], b[:, 1536:1728], a[:, :768]],
@@ -523,15 +541,15 @@
 
 
 def collect_kernel(tensor_ref, *refs):
-    kept, got, attn, units, out_ref = refs[:4], refs[4:8], refs[8], refs[9], refs[10]
+    kept, got, second, out_ref = refs[:4], refs[4:8], refs[8], refs[9]
     p = [x[0].astype(f32) + y[0].astype(f32) for x, y in zip(kept, got)]
     first = [part[:, : ATTN_COLS[i]] for i, part in enumerate(p)]
     wide = [part[:, ATTN_COLS[i] :] for i, part in enumerate(p)]
     layers = [
         (first, wide),
         (
-            [attn[0, :, 384 * i : 384 * i + ATTN_COLS[i]].astype(f32) for i in range(4)],
-            [units[0, :, 768 * i : 768 * i + 768].astype(f32) for i in range(4)],
+            [second[0, :, 384 * i : 384 * i + ATTN_COLS[i]].astype(f32) for i in range(4)],
+            [second[0, :, 1664 + 768 * i : 2432 + 768 * i].astype(f32) for i in range(4)],
         ),
     ]
     for layer, (first, wide) in enumerate(layers):
@@ -578,7 +596,7 @@
 
 def scatter_end(kept, got, second):
     tensor = lax.axis_index("tensor").astype(jnp.int32).reshape(1)
-    rows = kernel_call(collect_kernel, "collect", [tensor, *kept, *got, *second], [((8, 24, 2368), bf16)], scalar=True)[0]
+    rows = kernel_call(collect_kernel, "collect", [tensor, *kept, *got, second], [((8, 24, 2368), bf16)], scalar=True)[0]
     rows = lax.all_to_all(rows, ("pipe", "tensor", "core"), 0, 0, tiled=True)
     shapes = [(1, 24, 384)] * 4 + [(1, 24, 1536)] * 2 + [(1, 2, 6)] * 2 + [(1, 24), (1, 2, 24)] + [(1, 24)] * 5
     return kernel_call(
@@ -642,10 +660,10 @@
     )
     x_second, active_first, slope_first = units_forward(middle_first, units_first, vec_first, up_bias_first)
     x_second, second = pin(x_second, second)
-    attn_own = place_blocks(where, second[0], False)
-    attn_own, units_rows = pin(attn_own, second[1])
+    attn_own = place_blocks(where, second, False)
+    attn_own, second = pin(attn_own, second)
     attn_peer = exchange(attn_own, "c")
-    units_own = place_blocks(where, units_rows, True)
+    units_own = place_blocks(where, second, True)
     attn_peer, units_own = pin(attn_peer, units_own)
     attn_second = attn_own, attn_peer
     units_second = units_own, exchange(units_own, "c")
@@ -659,13 +677,12 @@
     grad_middle, units_vec, up_bias_grad, units_placed = units_backward(
         grad_out, middle_second, active_second, slope_second, units_second, vec_second, where
     )
-    units_total = lax.psum_scatter(units_placed, shards, scatter_dimension=0, tiled=True)
-    second_grad, attn_placed = attention_backward(
+    second_grad, placed = attention_backward(
         grad_middle, x_second, heads_second, soft_second, mixed_second, attn_second, vec_second, units_vec,
-        up_bias_grad, place_back, where,
-    )
-    second_grad, attn_placed, shared = pin(second_grad, attn_placed, shared)
-    attn_total = lax.psum_scatter(attn_placed, shards, scatter_dimension=0, tiled=True)
+        up_bias_grad, place_back, where, units_placed,
+    )
+    second_grad, placed, shared = pin(second_grad, placed, shared)
+    second_total = lax.psum_scatter(placed, shards, scatter_dimension=0, tiled=True)
     section_output = order_outputs(shared)
 
     grad_middle, units_vec, up_bias_grad, units_own, units_peer = units_backward(
@@ -687,7 +704,7 @@
     kept, got = fold_both(groups, 0), send_parts(fold_both(groups, 1), 2)
     kept, got = fold_on(kept, got, 0, "fold_four"), send_parts(fold_on(kept, got, 1, "fold_four"), 1)
     kept, got = fold_on(kept, got, 0, "fold_two"), send_parts(fold_on(kept, got, 1, "fold_two"), 0)
-    return (section_output, input_grad, *scatter_end(kept, got, (attn_total, units_total)))
+    return (section_output, input_grad, *scatter_end(kept, got, second_total))
 
 
 def solution(mesh):

time: 432 us -> 369 us (0.85)
  waiting for transfers between devices: 196 us -> 129 us
    reduce_scatter x2 -> x1, waiting for transfers between devices: 82.9 us -> 12.6 us  [local(): lax.psum_scatter(placed, shards, scatter_dimension=0, tiled=True)]
    ppermute x42, waiting for transfers between devices: 67.1 us -> 91.7 us  [exchange(): return lax.ppermute(value, axis, [(i, i ^ flip) for i in range(size)])]
    all_gather x2 -> x1, waiting for transfers between devices: 20 us -> 0.01 us  [gather_start(): second = lax.all_gather(jnp.concatenate(pieces, -1), ('z', 'x'), axis=0)]
  transfers between devices with their start and end apart: 54 -> 52, of which waited for: 22 -> 22; matrix products, arithmetic and copies ran while one was open for 3% -> 3% of each run, Pallas kernels for 26% -> 31%
where the time goes in v1:
time: 369 us; the launch traced here: 362 us
  waiting for transfers between devices  129 us (35%)
  Pallas kernels  128 us (35%)
  starting transfers between devices  72.3 us (20%)
  between operations  14.8 us (4%)
  local copies, waits for them, and re-layouts  7.65 us (2%)
  matrix products  5.58 us (2%)
  other arithmetic  5 us (1%)
    pallas_call x15, Pallas kernels, kernel_call(): pl.pallas_call(kernel, name=name, out_shape=shapes, in_specs=specs, out_s...  109 us
    ppermute x42, waiting for transfers between devices, exchange(): return lax.ppermute(value, axis, [(i, i ^ flip) for i in range(size)])  91.7 us
    ppermute x42, starting transfers between devices, exchange(): return lax.ppermute(value, axis, [(i, i ^ flip) for i in range(size)])  54.6 us
    pallas_call x8, Pallas kernels, fold(): pl.pallas_call(functools.partial(fold_kernel, [len(bits) for _, bits in t...  18.4 us
    all_to_all x1, waiting for transfers between devices, gather_start(): rows = lax.all_to_all(rows, ('pipe', 'tensor', 'core'), 0, 0, tiled=True)  14.4 us
    reduce_scatter x1, waiting for transfers between devices, local(): lax.psum_scatter(placed, shards, scatter_dimension=0, tiled=True)  12.6 us
    all_to_all x1, waiting for transfers between devices, scatter_end(): rows = lax.all_to_all(rows, ('pipe', 'tensor', 'core'), 0, 0, tiled=True)  10.7 us
  transfers between devices with their start and end apart: 52, of which 22 were waited for; matrix products, arithmetic and copies ran while one was open for 3% of the time, Pallas kernels for 31%

profile of v1, /device:TPU:0, one launch (start us, length us, event | category | flops | bytes accessed | tf_op | source)
XLA Modules:
  0.0 362.3 jit_solution(17799620165529473988)
XLA Ops:
  9.4 4.6 %all-to-all-start = ((bf16[8,24,2368]{2,1,0:T(8,128)(2,1)}), bf16[8,24,2368]{2,1,0:T(8,128)(2,1)S(1)}, u32[]{:S(2)}, u32[]{:S(2)}) async-start(bf16[8,24,2368]{2,1,0:T(8,128)(2,1)} %pack.1), calls=%async_computation | async-start | bytes 1867776 | tf_op jit(solution)/shard_map/all_to_all | solution.py:438
  14.0 14.4 %all-to-all-done = bf16[8,24,2368]{2,1,0:T(8,128)(2,1)S(1)} async-done(((bf16[8,24,2368]{2,1,0:T(8,128)(2,1)}), bf16[8,24,2368]{2,1,0:T(8,128)(2,1)S(1)}, u32[]{:S(2)}, u32[]{:S(2)}) %all-to-all-start) | async-done | bytes 909344 | tf_op jit(solution)/shard_map/all_to_all | solution.py:438
  43.9 5.1 %collective-permute-done.1 = bf16[2,48,1152]{2,1,0:T(8,128)(2,1)S(1)} collective-permute-done((bf16[2,48,1152]{2,1,0:T(8,128)(2,1)S(1)}, bf16[2,48,1152]{2,1,0:T(8,128)(2,1)S(1)}, u32[]{:S(2)}, u32[]{:S(2)}) %collective-permute-start.1) | collective-permute-done | bytes 221216 | tf_op jit(solution)/shard_map/ppermute | solution.py:337
  49.3 4.4 %collective-permute-start.5 = (bf16[4,48,1152]{2,1,0:T(8,128)(2,1)S(1)}, bf16[4,48,1152]{2,1,0:T(8,128)(2,1)S(1)}, u32[]{:S(2)}, u32[]{:S(2)}) collective-permute-start(bf16[4,48,1152]{2,1,0:T(8,128)(2,1)S(1)} %pad_maximum_fusion.7), channel_id=1, source_target_pairs={{0,48},{16,32},{32,16},{48,0},{1,49},{17,33},{33,17},{49,1},{2,50}... | collective-permute-start | bytes 1327112 | tf_op jit(solution)/shard_map/ppermute | solution.py:337
  59.3 4.8 %collective-permute-done.2 = bf16[4,48,1152]{2,1,0:T(8,128)(2,1)S(1)} collective-permute-done((bf16[4,48,1152]{2,1,0:T(8,128)(2,1)S(1)}, bf16[4,48,1152]{2,1,0:T(8,128)(2,1)S(1)}, u32[]{:S(2)}, u32[]{:S(2)}) %collective-permute-start.2) | collective-permute-done | bytes 442400 | tf_op jit(solution)/shard_map/ppermute | solution.py:337
  70.7 31.0 %collective-permute-done.12.refs_4_.refs_9_.refs_10_ = bf16[8,48,1152]{2,1,0:T(8,128)(2,1)S(1)} collective-permute-done((bf16[8,48,1152]{2,1,0:T(8,128)(2,1)S(1)}, bf16[8,48,1152]{2,1,0:T(8,128)(2,1)S(1)}, u32[]{:S(2)}, u32[]{:S(2)}) %collective-permute-start.12) | collective-permute-done | bytes 884768 | tf_op jit(solution)/shard_map/ppermute | solution.py:337
  112.7 4.5 %assemble_units.1.own_ref.refs_4_ = bf16[4,768,768]{2,1,0:T(8,128)(2,1)} custom-call(bf16[8,48,1152]{2,1,0:T(8,128)(2,1)S(1)} %pad_maximum_fusion.1.refs_0_.refs_1_, bf16[8,48,1152]{2,1,0:T(8,128)(2,1)S(1)} %pad_maximum_fusion.1.refs_0_.refs_1_, bf16[8,48,1152]{2,1,0:T(8,128)(2,1)S(1)} %pad_maximum_fusion.2.refs_1_.refs_2_.refs_3_, ...), custom_call_target="tpu_custom_call" | custom-call | flops 1 | bytes 1 | tf_op jit(solution)/shard_map/assemble_units/pallas_call | solution.py:262
  119.7 8.6 %attention_forward.2 = (f32[192,768]{1,0:T(8,128)S(1)}, bf16[3,192,768]{2,1,0:T(8,128)(2,1)}, f32[12,192,192]{2,1,0:T(8,128)}, bf16[192,768]{1,0:T(8,128)(2,1)S(...) custom-call(s32[1]{0:T(128)} %bitcast.3.length_ref, bf16[192,768]{1,0:T(8,128)(2,1)S(1)} %fusion.7.x_ref.refs_1_, ...), custom_call_target="tpu_custom_call" | custom-call | flops 1 | bytes 1 | tf_op jit(solution)/shard_map/attention_forward/pallas_call | solution.py:262
  128.3 8.2 %units_forward.2 = (bf16[192,768]{1,0:T(8,128)(2,1)S(1)}, bf16[192,3072]{1,0:T(8,128)(2,1)}, f32[192,3072]{1,0:T(8,128)}) custom-call(f32[192,768]{1,0:T(8,128)S(1)} %get-tuple-element.125.middle_ref.refs_1_, bf16[4,768,768]{2,1,0:T(8,128)(2,1)} %assemble_units.1.own_ref.refs_4_, bf16[4,768,768]{2,1,0:T(8,128)(2,1)} %collective-permute-done.17.peer_ref.refs_5_, ...), custom_call_target="tpu_custom_call" | custom-call | flops 1 | bytes 1 | tf_op jit(solution)/shard_map/units_forward/pallas_call | solution.py:262
  136.4 4.8 %place_attention.1.own_ref.refs_6_ = bf16[768,1664]{1,0:T(8,128)(2,1)} custom-call(s32[2]{0:T(128)S(1)} %pad_add_fusion.chip_ref.refs_0_, bf16[16,48,4736]{2,1,0:T(8,128)(2,1)} %bitcast.154), custom_call_target="tpu_custom_call" | custom-call | flops 1 | bytes 1 | tf_op jit(solution)/shard_map/place_attention/pallas_call | solution.py:262
  141.6 5.6 %place_units.1.own_ref.refs_5_ = bf16[4,768,768]{2,1,0:T(8,128)(2,1)} custom-call(s32[2]{0:T(128)S(1)} %pad_add_fusion.chip_ref.refs_0_, bf16[16,48,4736]{2,1,0:T(8,128)(2,1)} %bitcast.155), custom_call_target="tpu_custom_call" | custom-call | flops 1 | bytes 1 | tf_op jit(solution)/shard_map/place_units/pallas_call | solution.py:262
  148.2 8.5 %attention_forward.3 = (f32[192,768]{1,0:T(8,128)S(1)}, bf16[3,192,768]{2,1,0:T(8,128)(2,1)}, f32[12,192,192]{2,1,0:T(8,128)}, bf16[192,768]{1,0:T(8,128)(2,1)S(...) custom-call(s32[1]{0:T(128)} %bitcast.3.length_ref, bf16[192,768]{1,0:T(8,128)(2,1)S(1)} %get-tuple-element.130.x_ref.refs_2_, ...), custom_call_target="tpu_custom_call" | custom-call | flops 1 | bytes 1 | tf_op jit(solution)/shard_map/attention_forward/pallas_call | solution.py:262
  156.7 8.2 %units_forward.3 = (bf16[192,768]{1,0:T(8,128)(2,1)S(1)}, bf16[192,3072]{1,0:T(8,128)(2,1)}, f32[192,3072]{1,0:T(8,128)}) custom-call(f32[192,768]{1,0:T(8,128)S(1)} %get-tuple-element.135.middle_ref.refs_2_, bf16[4,768,768]{2,1,0:T(8,128)(2,1)} %place_units.1.own_ref.refs_5_, bf16[4,768,768]{2,1,0:T(8,128)(2,1)} %collective-permute-done.19.peer_ref.refs_6_, ...), custom_call_target="tpu_custom_call" | custom-call | flops 1 | bytes 1 | tf_op jit(solution)/shard_map/units_forward/pallas_call | solution.py:262
  171.9 13.2 %units_backward.2 = (f32[192,768]{1,0:T(8,128)S(1)}, f32[8,768]{1,0:T(8,128)S(1)}, f32[1,3072]{1,0:T(1,128)S(1)}, bf16[32,48,4736]{2,1,0:T(8,128)(2,1)}) custom-call(s32[2]{0:T(128)S(1)} %pad_add_fusion.chip_ref.refs_0_, bf16[192,768]{1,0:T(8,128)(2,1)S(1)} %fusion.6.refs_1_, f32[192,768]{1,0:T(8,128)S(1)} %get-tuple-element.135.middle_ref.refs_2_, ...), custom_call_target="tpu_custom_call" | custom-call | flops 1 | bytes 1 | tf_op jit(solution)/shard_map/units_backward/pallas_call | solution.py:262
  185.1 14.2 %attention_backward.2 = (bf16[192,768]{1,0:T(8,128)(2,1)S(1)}, bf16[32,48,4736]{2,1,0:T(8,128)(2,1)}) custom-call(s32[2]{0:T(128)S(1)} %pad_add_fusion.chip_ref.refs_0_, f32[192,768]{1,0:T(8,128)S(1)} %get-tuple-element.141.refs_1_, bf16[192,768]{1,0:T(8,128)(2,1)S(1)} %get-tuple-element.130.x_ref.refs_2_, ...), custom_call_target="tpu_custom_call", output_to_operand_aliasing={{1}: (12, {})} | custom-call | flops 1 | bytes 1 | tf_op jit(solution)/shard_map/attention_backward/pallas_call | solution.py:262
  199.4 11.8 %units_backward.3 = (f32[192,768]{1,0:T(8,128)S(1)}, f32[8,768]{1,0:T(8,128)S(1)}, f32[1,3072]{1,0:T(1,128)S(1)}, bf16[4,16,48,768]{3,2,1,0:T(8,128)(2,1)}, bf16[4,16,48,768]{3,2,1,0:T(8,128)(2,1)}) custom-call(bf16[192,768]{1,0:T(8,128)(2,1)S(1)} %get-tuple-element.155.refs_0_, f32[192,768]{1,0:T(8,128)S(1)} %get-tuple-element.125.middle_ref.refs_1_, ...), custom_call_target="tpu_custom_call" | custom-call | flops 1 | bytes 1 | tf_op jit(solution)/shard_map/units_backward/pallas_call | solution.py:262
  211.2 14.4 %attention_backward.3 = (bf16[192,768]{1,0:T(8,128)(2,1)S(1)}, bf16[16,48,1664]{2,1,0:T(8,128)(2,1)}, bf16[16,48,1664]{2,1,0:T(8,128)(2,1)}) custom-call(f32[192,768]{1,0:T(8,128)S(1)} %get-tuple-element.158.refs_0_, bf16[192,768]{1,0:T(8,128)(2,1)S(1)} %fusion.7.x_ref.refs_1_, bf16[3,192,768]{2,1,0:T(8,128)(2,1)} %get-tuple-element.159.refs_2_, ...), custom_call_target="tpu_custom_call" | custom-call | flops 1 | bytes 1 | tf_op jit(solution)/shard_map/attention_backward/pallas_call | solution.py:262
  240.1 8.2 %collective-permute-done.32 = bf16[8,48,768]{2,1,0:T(8,128)(2,1)S(1)} collective-permute-done((bf16[8,48,768]{2,1,0:T(8,128)(2,1)S(1)}, bf16[8,48,768]{2,1,0:T(8,128)(2,1)S(1)}, u32[]{:S(2)}, u32[]{:S(2)}) %collective-permute-start.32) | collective-permute-done | bytes 589856 | tf_op jit(solution)/shard_map/ppermute | solution.py:337
  252.6 5.7 %collective-permute-done.28 = bf16[8,48,384]{2,1,0:T(8,128)(2,1)S(1)} collective-permute-done((bf16[8,48,384]{2,1,0:T(8,128)(2,1)S(1)}, bf16[8,48,384]{2,1,0:T(8,128)(2,1)S(1)}, u32[]{:S(2)}, u32[]{:S(2)}) %collective-permute-start.28) | collective-permute-done | bytes 294944 | tf_op jit(solution)/shard_map/ppermute | solution.py:337
  272.6 15.0 %collective-permute-done.36 = bf16[4,48,1152]{2,1,0:T(8,128)(2,1)S(1)} collective-permute-done((bf16[4,48,1152]{2,1,0:T(8,128)(2,1)S(1)}, bf16[4,48,1152]{2,1,0:T(8,128)(2,1)S(1)}, u32[]{:S(2)}, u32[]{:S(2)}) %collective-permute-start.36) | collective-permute-done | bytes 442400 | tf_op jit(solution)/shard_map/ppermute | solution.py:337
  299.6 7.7 %collective-permute-done.40 = bf16[2,48,1152]{2,1,0:T(8,128)(2,1)S(1)} collective-permute-done((bf16[2,48,1152]{2,1,0:T(8,128)(2,1)S(1)}, bf16[2,48,1152]{2,1,0:T(8,128)(2,1)S(1)}, u32[]{:S(2)}, u32[]{:S(2)}) %collective-permute-start.40) | collective-permute-done | bytes 221216 | tf_op jit(solution)/shard_map/ppermute | solution.py:337
  320.8 12.6 %reduce-scatter.2.cloned.1.call-done.refs_8_ = bf16[1,48,4736]{2,1,0:T(8,128)(2,1)} async-done(((bf16[32,48,4736]{2,1,0:T(8,128)(2,1)}), bf16[1,48,4736]{2,1,0:T(8,128)(2,1)}) %reduce-scatter.2.cloned.1.call-update) | async-done | bytes 454672 | tf_op jit(solution)/shard_map/reduce_scatter | solution.py:685
  335.6 4.4 %all-to-all-start.1 = ((bf16[8,24,2368]{2,1,0:T(8,128)(2,1)}), bf16[8,24,2368]{2,1,0:T(8,128)(2,1)S(1)}, u32[]{:S(2)}, u32[]{:S(2)}) async-start(bf16[8,24,2368]{2,1,0:T(8,128)(2,1)} %collect.1), calls=%async_computation.2 | async-start | bytes 1867776 | tf_op jit(solution)/shard_map/all_to_all | solution.py:600
  343.7 10.7 %all-to-all-done.1.rows_ref = bf16[8,24,2368]{2,1,0:T(8,128)(2,1)S(1)} async-done(((bf16[8,24,2368]{2,1,0:T(8,128)(2,1)}), bf16[8,24,2368]{2,1,0:T(8,128)(2,1)S(1)}, u32[]{:S(2)}, u32[]{:S(2)}) %all-to-all-start.1) | async-done | bytes 909344 | tf_op jit(solution)/shard_map/all_to_all | solution.py:600
  (194 shorter events, 117.1 us)
Async XLA Ops:
  9.4 19.0 %all-to-all-start = ((bf16[8,24,2368]{2,1,0:T(8,128)(2,1)}), bf16[8,24,2368]{2,1,0:T(8,128)(2,1)S(1)}, u32[]{:S(2)}, u32[]{:S(2)}) async-start(bf16[8,24,2368]{2,1,0:T(8,128)(2,1)} %pack.1), calls=%async_computation | async-start | bytes 1867776 | tf_op jit(solution)/shard_map/all_to_all | solution.py:438
  14.0 122.5 %all-gather.3.cloned.1.call-start = ((), (), s32[]{:S(2)}) async-start(), calls=%async_computation.4 | async-start | bytes 7729152 | tf_op jit(solution)/shard_map/all_gather | solution.py:447
  29.6 303.8 %reduce-scatter.2.cloned.1.call-start = ((), (), s32[]{:S(2)}) async-start(), calls=%async_computation.3 | async-start | bytes 15003648 | tf_op jit(solution)/shard_map/reduce_scatter | solution.py:685
  49.3 17.2 %collective-permute-start.5 = (bf16[4,48,1152]{2,1,0:T(8,128)(2,1)S(1)}, bf16[4,48,1152]{2,1,0:T(8,128)(2,1)S(1)}, u32[]{:S(2)}, u32[]{:S(2)}) collective-permute-start(bf16[4,48,1152]{2,1,0:T(8,128)(2,1)S(1)} %pad_maximum_fusion.7), channel_id=1, source_target_pairs={{0,48},{16,32},{32,16},{48,0},{1,49},{17,33},{33,17},{49,1},{2,50}... | collective-permute-start | bytes 1327112 | tf_op jit(solution)/shard_map/ppermute | solution.py:337
  64.3 37.4 %collective-permute-start.12 = (bf16[8,48,1152]{2,1,0:T(8,128)(2,1)S(1)}, bf16[8,48,1152]{2,1,0:T(8,128)(2,1)S(1)}, u32[]{:S(2)}, u32[]{:S(2)}) collective-permute-start(bf16[8,48,1152]{2,1,0:T(8,128)(2,1)S(1)} %pad_maximum_fusion.1.refs_0_.refs_1_), channel_id=1, source_target_pairs={{0,48},{16,32},{32,16},{48,0},{1,49},{17,33},{33,17},{49,1},{2,50}... | collective-permute-start | bytes 2654216 | tf_op jit(solution)/shard_map/ppermute | solution.py:337
  66.6 36.9 %collective-permute-start.13 = (bf16[8,48,1152]{2,1,0:T(8,128)(2,1)S(1)}, bf16[8,48,1152]{2,1,0:T(8,128)(2,1)S(1)}, u32[]{:S(2)}, u32[]{:S(2)}) collective-permute-start(bf16[8,48,1152]{2,1,0:T(8,128)(2,1)S(1)} %pad_maximum_fusion.2.refs_1_.refs_2_.refs_3_), channel_id=1, source_target_pairs={{0,16},{16,0},{32,48},{48,32},{1,17},{17,1},{33,49},{49,33},{2,18}... | collective-permute-start | bytes 2654216 | tf_op jit(solution)/shard_map/ppermute | solution.py:337
  67.0 41.4 %collective-permute-start.15 = (bf16[8,48,1280]{2,1,0:T(8,128)(2,1)S(1)}, bf16[8,48,1280]{2,1,0:T(8,128)(2,1)S(1)}, u32[]{:S(2)}, u32[]{:S(2)}) collective-permute-start(bf16[8,48,1280]{2,1,0:T(8,128)(2,1)S(1)} %pad_maximum_fusion.refs_3_.refs_6_.refs_7_.refs_8_), channel_id=1, source_target_pairs={{0,4},{4,0},{8,12},{12,8},{1,5},{5,1},{9,13},{13,9},{2,6},{6,2},{1... | collective-permute-start | bytes 2949128 | tf_op jit(solution)/shard_map/ppermute | solution.py:337
  68.3 38.6 %collective-permute-start.14 = (bf16[8,48,1152]{2,1,0:T(8,128)(2,1)S(1)}, bf16[8,48,1152]{2,1,0:T(8,128)(2,1)S(1)}, u32[]{:S(2)}, u32[]{:S(2)}) collective-permute-start(bf16[8,48,1152]{2,1,0:T(8,128)(2,1)S(1)} %pad_maximum_fusion.3.refs_2_.refs_4_.refs_5_), channel_id=1, source_target_pairs={{0,12},{4,8},{8,4},{12,0},{1,13},{5,9},{9,5},{13,1},{2,14},{6,10},... | collective-permute-start | bytes 2654216 | tf_op jit(solution)/shard_map/ppermute | solution.py:337
  165.6 33.8 %collective-permute-start.21 = (bf16[192,768]{1,0:T(8,128)(2,1)S(1)}, bf16[192,768]{1,0:T(8,128)(2,1)S(1)}, u32[]{:S(2)}, u32[]{:S(2)}) collective-permute-start(bf16[192,768]{1,0:T(8,128)(2,1)S(1)} %get-tuple-element.233), channel_id=1, source_target_pairs={{0,64},{64,0},{1,65},{65,1},{2,66},{66,2},{3,67},{67,3},{4,68},{68... | collective-permute-start | bytes 884744 | tf_op jit(solution)/shard_map/ppermute | solution.py:341
  166.4 33.0 %collective-permute-start.22 = (bf16[192,768]{1,0:T(8,128)(2,1)S(1)}, bf16[192,768]{1,0:T(8,128)(2,1)S(1)}, u32[]{:S(2)}, u32[]{:S(2)}) collective-permute-start(bf16[192,768]{1,0:T(8,128)(2,1)S(1)} %get-tuple-element.233), channel_id=1, source_target_pairs={{0,65},{1,64},{64,1},{65,0},{2,67},{3,66},{66,3},{67,2},{4,69},{5,... | collective-permute-start | bytes 884744 | tf_op jit(solution)/shard_map/ppermute | solution.py:345
  169.3 30.0 %collective-permute-start.20 = (bf16[192,768]{1,0:T(8,128)(2,1)S(1)}, bf16[192,768]{1,0:T(8,128)(2,1)S(1)}, u32[]{:S(2)}, u32[]{:S(2)}) collective-permute-start(bf16[192,768]{1,0:T(8,128)(2,1)S(1)} %get-tuple-element.151), channel_id=1, source_target_pairs={{0,1},{1,0},{2,3},{3,2},{4,5},{5,4},{6,7},{7,6},{8,9},{9,8},{10,11... | collective-permute-start | bytes 884744 | tf_op jit(solution)/shard_map/ppermute | solution.py:349
  231.0 17.3 %collective-permute-start.32 = (bf16[8,48,768]{2,1,0:T(8,128)(2,1)S(1)}, bf16[8,48,768]{2,1,0:T(8,128)(2,1)S(1)}, u32[]{:S(2)}, u32[]{:S(2)}) collective-permute-start(bf16[8,48,768]{2,1,0:T(8,128)(2,1)S(1)} %get-tuple-element.177), channel_id=1, source_target_pairs={{0,48},{16,32},{32,16},{48,0},{1,49},{17,33},{33,17},{49,1},{2,50}... | collective-permute-start | bytes 1769480 | tf_op jit(solution)/shard_map/ppermute | solution.py:337
  234.3 16.9 %collective-permute-start.33 = (bf16[8,48,768]{2,1,0:T(8,128)(2,1)S(1)}, bf16[8,48,768]{2,1,0:T(8,128)(2,1)S(1)}, u32[]{:S(2)}, u32[]{:S(2)}) collective-permute-start(bf16[8,48,768]{2,1,0:T(8,128)(2,1)S(1)} %get-tuple-element.178), channel_id=1, source_target_pairs={{0,16},{16,0},{32,48},{48,32},{1,17},{17,1},{33,49},{49,33},{2,18}... | collective-permute-start | bytes 1769480 | tf_op jit(solution)/shard_map/ppermute | solution.py:337
  234.4 16.9 %collective-permute-start.34 = (bf16[8,48,768]{2,1,0:T(8,128)(2,1)S(1)}, bf16[8,48,768]{2,1,0:T(8,128)(2,1)S(1)}, u32[]{:S(2)}, u32[]{:S(2)}) collective-permute-start(bf16[8,48,768]{2,1,0:T(8,128)(2,1)S(1)} %get-tuple-element.179), channel_id=1, source_target_pairs={{0,12},{4,8},{8,4},{12,0},{1,13},{5,9},{9,5},{13,1},{2,14},{6,10},... | collective-permute-start | bytes 1769480 | tf_op jit(solution)/shard_map/ppermute | solution.py:337
  236.0 16.5 %collective-permute-start.35 = (bf16[8,48,768]{2,1,0:T(8,128)(2,1)}, bf16[8,48,768]{2,1,0:T(8,128)(2,1)S(1)}, u32[]{:S(2)}, u32[]{:S(2)}) collective-permute-start(bf16[8,48,768]{2,1,0:T(8,128)(2,1)} %get-tuple-element.180), channel_id=1, source_target_pairs={{0,4},{4,0},{8,12},{12,8},{1,5},{5,1},{9,13},{13,9},{2,6},{6,2},{1... | collective-permute-start | bytes 1769480 | tf_op jit(solution)/shard_map/ppermute | solution.py:337
  238.1 22.8 %collective-permute-start.31 = (bf16[8,48,512]{2,1,0:T(8,128)(2,1)S(1)}, bf16[8,48,512]{2,1,0:T(8,128)(2,1)S(1)}, u32[]{:S(2)}, u32[]{:S(2)}) collective-permute-start(bf16[8,48,512]{2,1,0:T(8,128)(2,1)S(1)} %get-tuple-element.174), channel_id=1, source_target_pairs={{0,4},{4,0},{8,12},{12,8},{1,5},{5,1},{9,13},{13,9},{2,6},{6,2},{1... | collective-permute-start | bytes 1179656 | tf_op jit(solution)/shard_map/ppermute | solution.py:337
  265.0 25.4 %collective-permute-start.39 = (bf16[4,48,1280]{2,1,0:T(8,128)(2,1)}, bf16[4,48,1280]{2,1,0:T(8,128)(2,1)S(1)}, u32[]{:S(2)}, u32[]{:S(2)}) collective-permute-start(bf16[4,48,1280]{2,1,0:T(8,128)(2,1)} %get-tuple-element.188), channel_id=1, source_target_pairs={{0,12},{4,8},{8,4},{12,0},{1,13},{5,9},{9,5},{13,1},{2,14},{6,10},... | collective-permute-start | bytes 1474568 | tf_op jit(solution)/shard_map/ppermute | solution.py:337
  266.2 21.4 %collective-permute-start.36 = (bf16[4,48,1152]{2,1,0:T(8,128)(2,1)S(1)}, bf16[4,48,1152]{2,1,0:T(8,128)(2,1)S(1)}, u32[]{:S(2)}, u32[]{:S(2)}) collective-permute-start(bf16[4,48,1152]{2,1,0:T(8,128)(2,1)S(1)} %get-tuple-element.182), channel_id=1, source_target_pairs={{0,16},{16,0},{32,48},{48,32},{1,17},{17,1},{33,49},{49,33},{2,18}... | collective-permute-start | bytes 1327112 | tf_op jit(solution)/shard_map/ppermute | solution.py:337
  266.8 22.9 %collective-permute-start.37 = (bf16[4,48,1152]{2,1,0:T(8,128)(2,1)}, bf16[4,48,1152]{2,1,0:T(8,128)(2,1)S(1)}, u32[]{:S(2)}, u32[]{:S(2)}) collective-permute-start(bf16[4,48,1152]{2,1,0:T(8,128)(2,1)} %get-tuple-element.184), channel_id=1, source_target_pairs={{0,48},{16,32},{32,16},{48,0},{1,49},{17,33},{33,17},{49,1},{2,50}... | collective-permute-start | bytes 1327112 | tf_op jit(solution)/shard_map/ppermute | solution.py:337
  269.1 21.3 %collective-permute-start.38 = (bf16[4,48,1152]{2,1,0:T(8,128)(2,1)}, bf16[4,48,1152]{2,1,0:T(8,128)(2,1)S(1)}, u32[]{:S(2)}, u32[]{:S(2)}) collective-permute-start(bf16[4,48,1152]{2,1,0:T(8,128)(2,1)} %get-tuple-element.186), channel_id=1, source_target_pairs={{0,4},{4,0},{8,12},{12,8},{1,5},{5,1},{9,13},{13,9},{2,6},{6,2},{1... | collective-permute-start | bytes 1327112 | tf_op jit(solution)/shard_map/ppermute | solution.py:337
  315.6 25.6 %collective-permute-start.25 = (bf16[192,768]{1,0:T(8,128)(2,1)}, bf16[192,768]{1,0:T(8,128)(2,1)}, u32[]{:S(2)}, u32[]{:S(2)}) collective-permute-start(bf16[192,768]{1,0:T(8,128)(2,1)} %get-tuple-element.231), channel_id=1, source_target_pairs={{0,64},{64,0},{1,65},{65,1},{2,66},{66,2},{3,67},{67,3},{4,68},{68... | collective-permute-start | bytes 884744 | tf_op jit(solution)/shard_map/ppermute | solution.py:341
  317.7 23.5 %collective-permute-start.26 = (bf16[192,768]{1,0:T(8,128)(2,1)}, bf16[192,768]{1,0:T(8,128)(2,1)}, u32[]{:S(2)}, u32[]{:S(2)}) collective-permute-start(bf16[192,768]{1,0:T(8,128)(2,1)} %get-tuple-element.231), channel_id=1, source_target_pairs={{0,65},{1,64},{64,1},{65,0},{2,67},{3,66},{66,3},{67,2},{4,69},{5,... | collective-permute-start | bytes 884744 | tf_op jit(solution)/shard_map/ppermute | solution.py:345
  320.3 20.9 %collective-permute-start.24 = (bf16[192,768]{1,0:T(8,128)(2,1)}, bf16[192,768]{1,0:T(8,128)(2,1)}, u32[]{:S(2)}, u32[]{:S(2)}) collective-permute-start(bf16[192,768]{1,0:T(8,128)(2,1)} %get-tuple-element.232), channel_id=1, source_target_pairs={{0,1},{1,0},{2,3},{3,2},{4,5},{5,4},{6,7},{7,6},{8,9},{9,8},{10,11... | collective-permute-start | bytes 884744 | tf_op jit(solution)/shard_map/ppermute | solution.py:349
  335.6 18.8 %all-to-all-start.1 = ((bf16[8,24,2368]{2,1,0:T(8,128)(2,1)}), bf16[8,24,2368]{2,1,0:T(8,128)(2,1)S(1)}, u32[]{:S(2)}, u32[]{:S(2)}) async-start(bf16[8,24,2368]{2,1,0:T(8,128)(2,1)} %collect.1), calls=%async_computation.2 | async-start | bytes 1867776 | tf_op jit(solution)/shard_map/all_to_all | solution.py:600
  (49 other events, 571.2 us)
Sparse Core Ops, SparseCore 0:
  29.8 86.8 all-gather.2
  199.5 133.8 reduce-scatter.1
